TPU v7x, 32 devices: a whole 2x2x4 slice. The times are simulated.
32 devices in a mesh: groups: 2 (over x), src: 16 (over z, y, core).
Axes of the slice: x: 2, y: 2, z: 4, core: 2. Of those that a mesh axis runs over, the one named last changes fastest.
Arguments:
- layout_mask: int32 [512, 256], P('groups'), parts along dimension 0, may hold values 0 or 1
- source_coords: int32 [32, 2], P('src'), may hold values from -8 to 8
- source_weights: int32 [32], P('src'), may hold values from 1 to 8
- focus_steps: int32 [16], replicated, may hold values from -4 to 4
- pupil_taps: float32 [48], replicated, may hold values from 0.25 to 1.75
- blur_x: float32 [31], replicated, may hold values from 0 to 2
- blur_y: float32 [31], replicated, may hold values from 0 to 2
- blur_z: float32 [31], replicated, may hold values from 0 to 2
Outputs:
- intensity: float32 [8192, 256], P(('groups', 'src')), parts along dimension 0
- latent: float32 [8192, 256], P(('groups', 'src')), parts along dimension 0
There are 2 independent parts, one for each index of `groups`. A program takes and returns all parts, laid end to end along the dimension named above; an argument that names none is the same for every part. Nothing has to cross between parts.
All inputs are finite; a program needn't handle non-finite values.
Results may differ from a plain program's by a relative error of at most 0.0022.
Values sent between devices are 32-bit elements; how exact they have to be, the bound alone decides.
A program may use at most 64 MiB of HBM per device.

v0:
```python
import math

import jax
import jax.numpy as jnp
from jax import lax
from jax.sharding import PartitionSpec as P

two_pi = 2.0 * math.pi
defocus_scale = 0.8
dose_scale = 2.0


def extended_2(block, sides, width):
    for axis, dim in sides:
        count = lax.axis_size(axis)
        forward = [(i, i + 1) for i in range(count - 1)]
        backward = [(target, source) for source, target in forward]
        low = lax.ppermute(
            lax.slice_in_dim(block, block.shape[dim] - width, None, axis=dim), axis, forward
        )
        high = lax.ppermute(lax.slice_in_dim(block, 0, width, axis=dim), axis, backward)
        block = jnp.concatenate([low, block, high], axis=dim)
    return block


def passed_along(block, axis, distance):
    devices = range(lax.axis_size(axis))
    route = [(i - distance, i) for i in devices if i - distance in devices]
    return lax.ppermute(block, axis, route)


def tap_matrix(out_pos, extent, tilt_index, focus_step, pupil_taps):
    tap_count = pupil_taps.shape[0]
    centre = (tap_count - 1) / 2.0
    column_pos = jnp.arange(extent, dtype=jnp.int32)
    offset = column_pos[None, :] - out_pos[:, None] + tap_count // 2
    inside = (offset >= 0) & (offset < tap_count)
    clipped = jnp.clip(offset, 0, tap_count - 1)
    amplitude = jnp.take(pupil_taps, clipped) / math.sqrt(tap_count)
    relative = clipped.astype(jnp.float32) - centre
    phase_angle = (
        two_pi * tilt_index.astype(jnp.float32) * relative / tap_count
        + defocus_scale * focus_step.astype(jnp.float32) * (relative / centre) ** 2
    )
    real_part = jnp.where(inside, amplitude * jnp.cos(phase_angle), jnp.zeros_like(amplitude))
    imag_part = jnp.where(inside, amplitude * jnp.sin(phase_angle), jnp.zeros_like(amplitude))
    return (real_part.astype(jnp.bfloat16), imag_part.astype(jnp.bfloat16))


def field_power(mask_bf, row_pos, tilt_x, tilt_y, focus_step, pupil_taps):
    rows_tile, cols_tile = mask_bf.shape
    row_count = row_pos.shape[0]
    col_pos = jnp.arange(cols_tile, dtype=jnp.int32)
    rows_real, rows_imag = tap_matrix(row_pos, rows_tile, tilt_y, focus_step, pupil_taps)
    cols_real, cols_imag = tap_matrix(col_pos, cols_tile, tilt_x, focus_step, pupil_taps)
    stacked = jnp.concatenate([rows_real, rows_imag], axis=0)
    first_pass = jnp.dot(stacked, mask_bf, preferred_element_type=jnp.float32).astype(jnp.bfloat16)
    joined = jnp.concatenate([first_pass[:row_count], first_pass[row_count:]], axis=1)
    upper_half = jnp.concatenate([cols_real.T, cols_imag.T], axis=1)
    lower_half = jnp.concatenate([-cols_imag.T, cols_real.T], axis=1)
    pupil_cols = jnp.concatenate([upper_half, lower_half], axis=0)
    field_parts = jnp.dot(joined, pupil_cols, preferred_element_type=jnp.float32)
    return field_parts[:, :cols_tile] ** 2 + field_parts[:, cols_tile:] ** 2


def on_device(
    layout_mask, source_coords, source_weights, focus_steps, pupil_taps, blur_x, blur_y, blur_z
):
    rows_tile, cols_tile = layout_mask.shape
    planes = focus_steps.shape[0]
    devices = lax.axis_size("src")
    src_local = source_coords.shape[0]
    mask_bf = layout_mask.astype(jnp.bfloat16)
    own_rows = planes * rows_tile // devices
    per_plane = devices // planes
    factors = source_weights.astype(jnp.float32) / (4.0 * src_local * devices)
    row_pos = jnp.arange(rows_tile, dtype=jnp.int32)

    def plane_term(focus_step):
        running = jnp.zeros((rows_tile, cols_tile), jnp.float32)
        for source in range(src_local):
            power = field_power(
                mask_bf,
                row_pos,
                source_coords[source, 0],
                source_coords[source, 1],
                focus_step,
                pupil_taps,
            )
            running = running + factors[source] * power
        return running

    partial_sum = lax.map(plane_term, focus_steps).reshape(planes * rows_tile, cols_tile)
    intensity = lax.psum_scatter(partial_sum, "src", scatter_dimension=0, tiled=True)
    acid_level = 1.0 - jnp.exp(-dose_scale * intensity)
    width_x = blur_x.shape[0]
    half_x = width_x // 2
    padded = jnp.pad(acid_level, ((0, 0), (half_x, half_x)))
    along_x = jnp.zeros_like(acid_level)
    for tap_index in range(width_x):
        along_x = (
            along_x + blur_x[tap_index] / width_x * padded[:, tap_index : tap_index + cols_tile]
        )
    width_y = blur_y.shape[0]
    half_y = width_y // 2
    extended = extended_2(along_x, (("src", 0),), half_y)
    along_y = jnp.zeros_like(along_x)
    for tap_index in range(width_y):
        along_y = along_y + blur_y[tap_index] / width_y * extended[tap_index : tap_index + own_rows]
    latent = blur_z[planes - 1] / planes * along_y
    for plane_lag in range(1 - planes, planes):
        if plane_lag != 0:
            arrived = passed_along(along_y, "src", plane_lag * per_plane)
            latent = latent + blur_z[plane_lag + planes - 1] / planes * arrived
    return (intensity, latent)


def solution(mesh):
    in_specs = (P("groups", None), P("src", None), P("src"), P(), P(), P(), P(), P())
    out_specs = (P(("groups", "src"), None), P(("groups", "src"), None))
    return jax.shard_map(
        on_device, mesh=mesh, in_specs=in_specs, out_specs=out_specs, check_vma=False
    )
```

profile of v0, /device:TPU:0, one launch (start us, length us, event | category | flops | bytes accessed | tf_op | source)
XLA Modules:
  0.0 1103.0 jit_solution(13562147983475835454)
XLA Ops:
  12.8 772.8 %while.15 = (s32[]{:T(128)}, f32[16,256,256]{2,1,0:T(8,128)}, f32[2]{0:T(128)S(1)}, f32[48]{0:T(128)}, f32[]{:T(128)}, /*index=5*/s32[16]{0:T(128)}, bf16[256,25...) while((s32[]{:T(128)}, f32[16,256,256]{2,1,0:T(8,128)}, ...), condition=%wide.region_1.3_spmd.clone.clone, body=%wide.region_0.2_spmd.clone.clone.sunk | while | flops 421986304 | bytes 8128281 | solution.py:93
  20.6 31.1 %select_convert_fusion.10 = (bf16[256,256]{1,0:T(8,128)(2,1)S(1)}, f32[256,256]{1,0:T(8,128)S(1)}) fusion(f32[]{:T(128)} %bitcast.270, f32[]{:T(128)} %get-tuple-element.654, f32[]{:T(128)} %bitcast.271, f32[]{:T(128)} %bitcast.272, f32[]{:T(128)} %bitcast.273, f32[]{:T(128)} %bitcast.274, f32[]{:T(128)} %bitcast.275, f32[]{:T(128)} %bitcast.276, ...), kind=kLoop, calls=%fused_computation.56.clone.1 | loop fusion | flops 7798784 | bytes 393416 | tf_op jit(solution)/shard_map/while/body/eval_jaxpr/convert_element_type | solution.py:47
  51.7 3.9 select_convert_fusion.11
  59.0 2.1 fusion.302
  68.9 31.1 %select_convert_fusion.10 = (bf16[256,256]{1,0:T(8,128)(2,1)S(1)}, f32[256,256]{1,0:T(8,128)S(1)}) fusion(f32[]{:T(128)} %bitcast.270, f32[]{:T(128)} %get-tuple-element.654, f32[]{:T(128)} %bitcast.271, f32[]{:T(128)} %bitcast.272, f32[]{:T(128)} %bitcast.273, f32[]{:T(128)} %bitcast.274, f32[]{:T(128)} %bitcast.275, f32[]{:T(128)} %bitcast.276, ...), kind=kLoop, calls=%fused_computation.56.clone.1 | loop fusion | flops 7798784 | bytes 393416 | tf_op jit(solution)/shard_map/while/body/eval_jaxpr/convert_element_type | solution.py:47
  100.0 3.9 select_convert_fusion.11
  117.2 31.1 %select_convert_fusion.10 = (bf16[256,256]{1,0:T(8,128)(2,1)S(1)}, f32[256,256]{1,0:T(8,128)S(1)}) fusion(f32[]{:T(128)} %bitcast.270, f32[]{:T(128)} %get-tuple-element.654, f32[]{:T(128)} %bitcast.271, f32[]{:T(128)} %bitcast.272, f32[]{:T(128)} %bitcast.273, f32[]{:T(128)} %bitcast.274, f32[]{:T(128)} %bitcast.275, f32[]{:T(128)} %bitcast.276, ...), kind=kLoop, calls=%fused_computation.56.clone.1 | loop fusion | flops 7798784 | bytes 393416 | tf_op jit(solution)/shard_map/while/body/eval_jaxpr/convert_element_type | solution.py:47
  148.3 3.9 select_convert_fusion.11
  155.6 2.1 fusion.302
  165.5 31.1 %select_convert_fusion.10 = (bf16[256,256]{1,0:T(8,128)(2,1)S(1)}, f32[256,256]{1,0:T(8,128)S(1)}) fusion(f32[]{:T(128)} %bitcast.270, f32[]{:T(128)} %get-tuple-element.654, f32[]{:T(128)} %bitcast.271, f32[]{:T(128)} %bitcast.272, f32[]{:T(128)} %bitcast.273, f32[]{:T(128)} %bitcast.274, f32[]{:T(128)} %bitcast.275, f32[]{:T(128)} %bitcast.276, ...), kind=kLoop, calls=%fused_computation.56.clone.1 | loop fusion | flops 7798784 | bytes 393416 | tf_op jit(solution)/shard_map/while/body/eval_jaxpr/convert_element_type | solution.py:47
  196.6 3.9 select_convert_fusion.11
  203.9 2.1 fusion.302
  213.8 31.1 %select_convert_fusion.10 = (bf16[256,256]{1,0:T(8,128)(2,1)S(1)}, f32[256,256]{1,0:T(8,128)S(1)}) fusion(f32[]{:T(128)} %bitcast.270, f32[]{:T(128)} %get-tuple-element.654, f32[]{:T(128)} %bitcast.271, f32[]{:T(128)} %bitcast.272, f32[]{:T(128)} %bitcast.273, f32[]{:T(128)} %bitcast.274, f32[]{:T(128)} %bitcast.275, f32[]{:T(128)} %bitcast.276, ...), kind=kLoop, calls=%fused_computation.56.clone.1 | loop fusion | flops 7798784 | bytes 393416 | tf_op jit(solution)/shard_map/while/body/eval_jaxpr/convert_element_type | solution.py:47
  244.9 3.9 select_convert_fusion.11
  252.2 2.1 fusion.302
  262.1 31.1 %select_convert_fusion.10 = (bf16[256,256]{1,0:T(8,128)(2,1)S(1)}, f32[256,256]{1,0:T(8,128)S(1)}) fusion(f32[]{:T(128)} %bitcast.270, f32[]{:T(128)} %get-tuple-element.654, f32[]{:T(128)} %bitcast.271, f32[]{:T(128)} %bitcast.272, f32[]{:T(128)} %bitcast.273, f32[]{:T(128)} %bitcast.274, f32[]{:T(128)} %bitcast.275, f32[]{:T(128)} %bitcast.276, ...), kind=kLoop, calls=%fused_computation.56.clone.1 | loop fusion | flops 7798784 | bytes 393416 | tf_op jit(solution)/shard_map/while/body/eval_jaxpr/convert_element_type | solution.py:47
  293.2 3.9 select_convert_fusion.11
  300.5 2.1 fusion.302
  310.4 31.1 %select_convert_fusion.10 = (bf16[256,256]{1,0:T(8,128)(2,1)S(1)}, f32[256,256]{1,0:T(8,128)S(1)}) fusion(f32[]{:T(128)} %bitcast.270, f32[]{:T(128)} %get-tuple-element.654, f32[]{:T(128)} %bitcast.271, f32[]{:T(128)} %bitcast.272, f32[]{:T(128)} %bitcast.273, f32[]{:T(128)} %bitcast.274, f32[]{:T(128)} %bitcast.275, f32[]{:T(128)} %bitcast.276, ...), kind=kLoop, calls=%fused_computation.56.clone.1 | loop fusion | flops 7798784 | bytes 393416 | tf_op jit(solution)/shard_map/while/body/eval_jaxpr/convert_element_type | solution.py:47
  341.5 3.9 select_convert_fusion.11
  358.7 31.1 %select_convert_fusion.10 = (bf16[256,256]{1,0:T(8,128)(2,1)S(1)}, f32[256,256]{1,0:T(8,128)S(1)}) fusion(f32[]{:T(128)} %bitcast.270, f32[]{:T(128)} %get-tuple-element.654, f32[]{:T(128)} %bitcast.271, f32[]{:T(128)} %bitcast.272, f32[]{:T(128)} %bitcast.273, f32[]{:T(128)} %bitcast.274, f32[]{:T(128)} %bitcast.275, f32[]{:T(128)} %bitcast.276, ...), kind=kLoop, calls=%fused_computation.56.clone.1 | loop fusion | flops 7798784 | bytes 393416 | tf_op jit(solution)/shard_map/while/body/eval_jaxpr/convert_element_type | solution.py:47
  389.8 3.9 select_convert_fusion.11
  406.9 31.1 %select_convert_fusion.10 = (bf16[256,256]{1,0:T(8,128)(2,1)S(1)}, f32[256,256]{1,0:T(8,128)S(1)}) fusion(f32[]{:T(128)} %bitcast.270, f32[]{:T(128)} %get-tuple-element.654, f32[]{:T(128)} %bitcast.271, f32[]{:T(128)} %bitcast.272, f32[]{:T(128)} %bitcast.273, f32[]{:T(128)} %bitcast.274, f32[]{:T(128)} %bitcast.275, f32[]{:T(128)} %bitcast.276, ...), kind=kLoop, calls=%fused_computation.56.clone.1 | loop fusion | flops 7798784 | bytes 393416 | tf_op jit(solution)/shard_map/while/body/eval_jaxpr/convert_element_type | solution.py:47
  438.1 3.9 select_convert_fusion.11
  445.4 2.1 fusion.302
  455.3 31.1 %select_convert_fusion.10 = (bf16[256,256]{1,0:T(8,128)(2,1)S(1)}, f32[256,256]{1,0:T(8,128)S(1)}) fusion(f32[]{:T(128)} %bitcast.270, f32[]{:T(128)} %get-tuple-element.654, f32[]{:T(128)} %bitcast.271, f32[]{:T(128)} %bitcast.272, f32[]{:T(128)} %bitcast.273, f32[]{:T(128)} %bitcast.274, f32[]{:T(128)} %bitcast.275, f32[]{:T(128)} %bitcast.276, ...), kind=kLoop, calls=%fused_computation.56.clone.1 | loop fusion | flops 7798784 | bytes 393416 | tf_op jit(solution)/shard_map/while/body/eval_jaxpr/convert_element_type | solution.py:47
  486.4 3.9 select_convert_fusion.11
  493.7 2.1 fusion.302
  503.6 31.1 %select_convert_fusion.10 = (bf16[256,256]{1,0:T(8,128)(2,1)S(1)}, f32[256,256]{1,0:T(8,128)S(1)}) fusion(f32[]{:T(128)} %bitcast.270, f32[]{:T(128)} %get-tuple-element.654, f32[]{:T(128)} %bitcast.271, f32[]{:T(128)} %bitcast.272, f32[]{:T(128)} %bitcast.273, f32[]{:T(128)} %bitcast.274, f32[]{:T(128)} %bitcast.275, f32[]{:T(128)} %bitcast.276, ...), kind=kLoop, calls=%fused_computation.56.clone.1 | loop fusion | flops 7798784 | bytes 393416 | tf_op jit(solution)/shard_map/while/body/eval_jaxpr/convert_element_type | solution.py:47
  534.7 3.9 select_convert_fusion.11
  542.0 2.1 fusion.302
  551.8 31.1 %select_convert_fusion.10 = (bf16[256,256]{1,0:T(8,128)(2,1)S(1)}, f32[256,256]{1,0:T(8,128)S(1)}) fusion(f32[]{:T(128)} %bitcast.270, f32[]{:T(128)} %get-tuple-element.654, f32[]{:T(128)} %bitcast.271, f32[]{:T(128)} %bitcast.272, f32[]{:T(128)} %bitcast.273, f32[]{:T(128)} %bitcast.274, f32[]{:T(128)} %bitcast.275, f32[]{:T(128)} %bitcast.276, ...), kind=kLoop, calls=%fused_computation.56.clone.1 | loop fusion | flops 7798784 | bytes 393416 | tf_op jit(solution)/shard_map/while/body/eval_jaxpr/convert_element_type | solution.py:47
  583.0 3.9 select_convert_fusion.11
  600.1 31.1 %select_convert_fusion.10 = (bf16[256,256]{1,0:T(8,128)(2,1)S(1)}, f32[256,256]{1,0:T(8,128)S(1)}) fusion(f32[]{:T(128)} %bitcast.270, f32[]{:T(128)} %get-tuple-element.654, f32[]{:T(128)} %bitcast.271, f32[]{:T(128)} %bitcast.272, f32[]{:T(128)} %bitcast.273, f32[]{:T(128)} %bitcast.274, f32[]{:T(128)} %bitcast.275, f32[]{:T(128)} %bitcast.276, ...), kind=kLoop, calls=%fused_computation.56.clone.1 | loop fusion | flops 7798784 | bytes 393416 | tf_op jit(solution)/shard_map/while/body/eval_jaxpr/convert_element_type | solution.py:47
  631.3 3.9 select_convert_fusion.11
  648.4 31.1 %select_convert_fusion.10 = (bf16[256,256]{1,0:T(8,128)(2,1)S(1)}, f32[256,256]{1,0:T(8,128)S(1)}) fusion(f32[]{:T(128)} %bitcast.270, f32[]{:T(128)} %get-tuple-element.654, f32[]{:T(128)} %bitcast.271, f32[]{:T(128)} %bitcast.272, f32[]{:T(128)} %bitcast.273, f32[]{:T(128)} %bitcast.274, f32[]{:T(128)} %bitcast.275, f32[]{:T(128)} %bitcast.276, ...), kind=kLoop, calls=%fused_computation.56.clone.1 | loop fusion | flops 7798784 | bytes 393416 | tf_op jit(solution)/shard_map/while/body/eval_jaxpr/convert_element_type | solution.py:47
  679.6 3.9 select_convert_fusion.11
  686.9 2.1 fusion.302
  696.7 31.1 %select_convert_fusion.10 = (bf16[256,256]{1,0:T(8,128)(2,1)S(1)}, f32[256,256]{1,0:T(8,128)S(1)}) fusion(f32[]{:T(128)} %bitcast.270, f32[]{:T(128)} %get-tuple-element.654, f32[]{:T(128)} %bitcast.271, f32[]{:T(128)} %bitcast.272, f32[]{:T(128)} %bitcast.273, f32[]{:T(128)} %bitcast.274, f32[]{:T(128)} %bitcast.275, f32[]{:T(128)} %bitcast.276, ...), kind=kLoop, calls=%fused_computation.56.clone.1 | loop fusion | flops 7798784 | bytes 393416 | tf_op jit(solution)/shard_map/while/body/eval_jaxpr/convert_element_type | solution.py:47
  727.9 3.9 select_convert_fusion.11
  735.1 2.1 fusion.302
  745.0 31.1 %select_convert_fusion.10 = (bf16[256,256]{1,0:T(8,128)(2,1)S(1)}, f32[256,256]{1,0:T(8,128)S(1)}) fusion(f32[]{:T(128)} %bitcast.270, f32[]{:T(128)} %get-tuple-element.654, f32[]{:T(128)} %bitcast.271, f32[]{:T(128)} %bitcast.272, f32[]{:T(128)} %bitcast.273, f32[]{:T(128)} %bitcast.274, f32[]{:T(128)} %bitcast.275, f32[]{:T(128)} %bitcast.276, ...), kind=kLoop, calls=%fused_computation.56.clone.1 | loop fusion | flops 7798784 | bytes 393416 | tf_op jit(solution)/shard_map/while/body/eval_jaxpr/convert_element_type | solution.py:47
  776.2 3.9 select_convert_fusion.11
  783.5 2.1 fusion.302
  807.8 53.0 %reduce-scatter.2.cloned.1.call-done = f32[256,256]{1,0:T(8,128)} async-done(((f32[4096,256]{1,0:T(8,128)}), f32[256,256]{1,0:T(8,128)}) %reduce-scatter.2.cloned.1.call-update) | async-done | bytes 262160 | tf_op jit(solution)/shard_map/reduce_scatter | solution.py:94
  861.8 2.1 fusion.153
  865.2 3.0 collective-permute-start
  889.0 3.1 collective-permute-start.31
  899.4 4.4 collective-permute-done.30
  905.1 4.3 collective-permute-done.29
  910.7 4.4 collective-permute-done.28
  916.4 4.3 collective-permute-done.27
  922.0 4.3 collective-permute-done.26
  926.3 20.7 %collective-permute-start.21 = (f32[256,256]{1,0:T(8,128)S(1)}, f32[256,256]{1,0:T(8,128)S(1)}, u32[]{:S(2)}, u32[]{:S(2)}) collective-permute-start(f32[256,256]{1,0:T(8,128)S(1)} %fusion.164), channel_id=1, source_target_pairs={{0,5},{1,6},{2,7},{3,8},{4,9},{5,10},{6,11},{7,12},{8,13},{9,14},{... | collective-permute-start | bytes 786440 | tf_op jit(solution)/shard_map/ppermute | solution.py:29
  947.0 11.3 %collective-permute-start.20 = (f32[256,256]{1,0:T(8,128)S(1)}, f32[256,256]{1,0:T(8,128)S(1)}, u32[]{:S(2)}, u32[]{:S(2)}) collective-permute-start(f32[256,256]{1,0:T(8,128)S(1)} %fusion.164), channel_id=1, source_target_pairs={{0,4},{1,5},{2,6},{3,7},{4,8},{5,9},{6,10},{7,11},{8,12},{9,13},{1... | collective-permute-start | bytes 786440 | tf_op jit(solution)/shard_map/ppermute | solution.py:29
  959.7 4.6 collective-permute-start.18
  964.3 3.1 collective-permute-start.17
  973.9 2.1 collective-permute-done.16
  977.3 8.7 collective-permute-done.15
  987.3 2.1 collective-permute-done.14
  990.7 14.2 %collective-permute-done.13 = f32[256,256]{1,0:T(8,128)S(1)} collective-permute-done((f32[256,256]{1,0:T(8,128)S(1)}, f32[256,256]{1,0:T(8,128)S(1)}, u32[]{:S(2)}, u32[]{:S(2)}) %collective-permute-start.13) | collective-permute-done | bytes 262176 | tf_op jit(solution)/shard_map/ppermute | solution.py:29
  1007.5 5.0 collective-permute-done.11
  1015.2 51.0 %collective-permute-done.9 = f32[256,256]{1,0:T(8,128)S(1)} collective-permute-done((f32[256,256]{1,0:T(8,128)S(1)}, f32[256,256]{1,0:T(8,128)S(1)}, u32[]{:S(2)}, u32[]{:S(2)}) %collective-permute-start.9) | collective-permute-done | bytes 262176 | tf_op jit(solution)/shard_map/ppermute | solution.py:29
  1067.4 3.9 collective-permute-done.8
  (249 shorter events, 222.7 us)
Async XLA Ops:
  7.2 853.6 %reduce-scatter.2.cloned.1.call-start = ((), (), s32[]{:S(2)}) async-start(), calls=%async_computation.1 | async-start | bytes 4456448 | tf_op jit(solution)/shard_map/reduce_scatter | solution.py:94
  785.6 0.7 copy-start
  785.6 21.5 %copy-start.1 = (f32[31]{0:T(128)S(1)}, f32[31]{0:T(128)}, u32[]{:S(2)}) copy-start(f32[31]{0:T(128)} %param.18) | copy-start | bytes 376
  785.6 288.4 %copy-start.2 = (f32[31]{0:T(128)S(1)}, f32[31]{0:T(128)}, u32[]{:S(2)}) copy-start(f32[31]{0:T(128)} %param.19) | copy-start | bytes 376
  863.9 24.3 %collective-permute-start.1 = (f32[15,256]{1,0:T(8,128)S(1)}, f32[15,256]{1,0:T(8,128)S(1)}, u32[]{:S(2)}, u32[]{:S(2)}) collective-permute-start(f32[15,256]{1,0:T(8,128)S(1)} %get-tuple-element.337), channel_id=1, source_target_pairs={{1,0},{2,1},{3,2},{4,3},{5,4},{6,5},{7,6},{8,7},{9,8},{10,9},{11,1... | collective-permute-start | bytes 46088 | tf_op jit(solution)/shard_map/ppermute | solution.py:21
  865.2 23.1 %collective-permute-start = (f32[15,256]{1,0:T(8,128)S(1)}, f32[15,256]{1,0:T(8,128)S(1)}, u32[]{:S(2)}, u32[]{:S(2)}) collective-permute-start(f32[15,256]{1,0:T(8,128)S(1)} %get-tuple-element.336), channel_id=1, source_target_pairs={{0,1},{1,2},{2,3},{3,4},{4,5},{5,6},{6,7},{7,8},{8,9},{9,10},{10,1... | collective-permute-start | bytes 46088 | tf_op jit(solution)/shard_map/ppermute | solution.py:18
  889.0 9.1 collective-permute-start.31
  892.2 11.6 %collective-permute-start.30 = (f32[256,256]{1,0:T(8,128)S(1)}, f32[256,256]{1,0:T(8,128)S(1)}, u32[]{:S(2)}, u32[]{:S(2)}) collective-permute-start(f32[256,256]{1,0:T(8,128)S(1)} %fusion.164), channel_id=1, source_target_pairs={{0,14},{1,15},{16,30},{17,31}} | collective-permute-start | bytes 786440 | tf_op jit(solution)/shard_map/ppermute | solution.py:29
  893.8 15.6 %collective-permute-start.29 = (f32[256,256]{1,0:T(8,128)S(1)}, f32[256,256]{1,0:T(8,128)S(1)}, u32[]{:S(2)}, u32[]{:S(2)}) collective-permute-start(f32[256,256]{1,0:T(8,128)S(1)} %fusion.164), channel_id=1, source_target_pairs={{0,13},{1,14},{2,15},{16,29},{17,30},{18,31}} | collective-permute-start | bytes 786440 | tf_op jit(solution)/shard_map/ppermute | solution.py:29
  895.2 19.9 %collective-permute-start.28 = (f32[256,256]{1,0:T(8,128)S(1)}, f32[256,256]{1,0:T(8,128)S(1)}, u32[]{:S(2)}, u32[]{:S(2)}) collective-permute-start(f32[256,256]{1,0:T(8,128)S(1)} %fusion.164), channel_id=1, source_target_pairs={{0,12},{1,13},{2,14},{3,15},{16,28},{17,29},{18,30},{19,31}} | collective-permute-start | bytes 786440 | tf_op jit(solution)/shard_map/ppermute | solution.py:29
  896.5 24.2 %collective-permute-start.27 = (f32[256,256]{1,0:T(8,128)S(1)}, f32[256,256]{1,0:T(8,128)S(1)}, u32[]{:S(2)}, u32[]{:S(2)}) collective-permute-start(f32[256,256]{1,0:T(8,128)S(1)} %fusion.164), channel_id=1, source_target_pairs={{0,11},{1,12},{2,13},{3,14},{4,15},{16,27},{17,28},{18,29},{19,30}... | collective-permute-start | bytes 786440 | tf_op jit(solution)/shard_map/ppermute | solution.py:29
  898.1 28.2 %collective-permute-start.26 = (f32[256,256]{1,0:T(8,128)S(1)}, f32[256,256]{1,0:T(8,128)S(1)}, u32[]{:S(2)}, u32[]{:S(2)}) collective-permute-start(f32[256,256]{1,0:T(8,128)S(1)} %fusion.164), channel_id=1, source_target_pairs={{0,10},{1,11},{2,12},{3,13},{4,14},{5,15},{16,26},{17,27},{18,28},... | collective-permute-start | bytes 786440 | tf_op jit(solution)/shard_map/ppermute | solution.py:29
  903.8 43.2 %collective-permute-start.25 = (f32[256,256]{1,0:T(8,128)S(1)}, f32[256,256]{1,0:T(8,128)S(1)}, u32[]{:S(2)}, u32[]{:S(2)}) collective-permute-start(f32[256,256]{1,0:T(8,128)S(1)} %fusion.164), channel_id=1, source_target_pairs={{0,9},{1,10},{2,11},{3,12},{4,13},{5,14},{6,15},{16,25},{17,26},{1... | collective-permute-start | bytes 786440 | tf_op jit(solution)/shard_map/ppermute | solution.py:29
  909.4 49.0 %collective-permute-start.24 = (f32[256,256]{1,0:T(8,128)S(1)}, f32[256,256]{1,0:T(8,128)S(1)}, u32[]{:S(2)}, u32[]{:S(2)}) collective-permute-start(f32[256,256]{1,0:T(8,128)S(1)} %fusion.164), channel_id=1, source_target_pairs={{0,8},{1,9},{2,10},{3,11},{4,12},{5,13},{6,14},{7,15},{16,24},{17,... | collective-permute-start | bytes 786440 | tf_op jit(solution)/shard_map/ppermute | solution.py:29
  915.1 44.6 %collective-permute-start.23 = (f32[256,256]{1,0:T(8,128)S(1)}, f32[256,256]{1,0:T(8,128)S(1)}, u32[]{:S(2)}, u32[]{:S(2)}) collective-permute-start(f32[256,256]{1,0:T(8,128)S(1)} %fusion.164), channel_id=1, source_target_pairs={{0,7},{1,8},{2,9},{3,10},{4,11},{5,12},{6,13},{7,14},{8,15},{16,23... | collective-permute-start | bytes 786440 | tf_op jit(solution)/shard_map/ppermute | solution.py:29
  920.7 43.6 %collective-permute-start.22 = (f32[256,256]{1,0:T(8,128)S(1)}, f32[256,256]{1,0:T(8,128)S(1)}, u32[]{:S(2)}, u32[]{:S(2)}) collective-permute-start(f32[256,256]{1,0:T(8,128)S(1)} %fusion.164), channel_id=1, source_target_pairs={{0,6},{1,7},{2,8},{3,9},{4,10},{5,11},{6,12},{7,13},{8,14},{9,15},... | collective-permute-start | bytes 786440 | tf_op jit(solution)/shard_map/ppermute | solution.py:29
  926.3 41.1 %collective-permute-start.21 = (f32[256,256]{1,0:T(8,128)S(1)}, f32[256,256]{1,0:T(8,128)S(1)}, u32[]{:S(2)}, u32[]{:S(2)}) collective-permute-start(f32[256,256]{1,0:T(8,128)S(1)} %fusion.164), channel_id=1, source_target_pairs={{0,5},{1,6},{2,7},{3,8},{4,9},{5,10},{6,11},{7,12},{8,13},{9,14},{... | collective-permute-start | bytes 786440 | tf_op jit(solution)/shard_map/ppermute | solution.py:29
  947.0 21.7 %collective-permute-start.20 = (f32[256,256]{1,0:T(8,128)S(1)}, f32[256,256]{1,0:T(8,128)S(1)}, u32[]{:S(2)}, u32[]{:S(2)}) collective-permute-start(f32[256,256]{1,0:T(8,128)S(1)} %fusion.164), channel_id=1, source_target_pairs={{0,4},{1,5},{2,6},{3,7},{4,8},{5,9},{6,10},{7,11},{8,12},{9,13},{1... | collective-permute-start | bytes 786440 | tf_op jit(solution)/shard_map/ppermute | solution.py:29
  958.4 11.6 %collective-permute-start.19 = (f32[256,256]{1,0:T(8,128)S(1)}, f32[256,256]{1,0:T(8,128)S(1)}, u32[]{:S(2)}, u32[]{:S(2)}) collective-permute-start(f32[256,256]{1,0:T(8,128)S(1)} %fusion.164), channel_id=1, source_target_pairs={{0,3},{1,4},{2,5},{3,6},{4,7},{5,8},{6,9},{7,10},{8,11},{9,12},{10... | collective-permute-start | bytes 786440 | tf_op jit(solution)/shard_map/ppermute | solution.py:29
  959.7 11.6 %collective-permute-start.18 = (f32[256,256]{1,0:T(8,128)S(1)}, f32[256,256]{1,0:T(8,128)S(1)}, u32[]{:S(2)}, u32[]{:S(2)}) collective-permute-start(f32[256,256]{1,0:T(8,128)S(1)} %fusion.164), channel_id=1, source_target_pairs={{0,2},{1,3},{2,4},{3,5},{4,6},{5,7},{6,8},{7,9},{8,10},{9,11},{10,... | collective-permute-start | bytes 786440 | tf_op jit(solution)/shard_map/ppermute | solution.py:29
  964.3 8.3 collective-permute-start.17
  967.4 8.7 collective-permute-start.16
  968.7 17.3 %collective-permute-start.15 = (f32[256,256]{1,0:T(8,128)S(1)}, f32[256,256]{1,0:T(8,128)S(1)}, u32[]{:S(2)}, u32[]{:S(2)}) collective-permute-start(f32[256,256]{1,0:T(8,128)S(1)} %fusion.164), channel_id=1, source_target_pairs={{2,0},{3,1},{4,2},{5,3},{6,4},{7,5},{8,6},{9,7},{10,8},{11,9},{12,... | collective-permute-start | bytes 786440 | tf_op jit(solution)/shard_map/ppermute | solution.py:29
  970.0 19.4 %collective-permute-start.14 = (f32[256,256]{1,0:T(8,128)S(1)}, f32[256,256]{1,0:T(8,128)S(1)}, u32[]{:S(2)}, u32[]{:S(2)}) collective-permute-start(f32[256,256]{1,0:T(8,128)S(1)} %fusion.164), channel_id=1, source_target_pairs={{3,0},{4,1},{5,2},{6,3},{7,4},{8,5},{9,6},{10,7},{11,8},{12,9},{13... | collective-permute-start | bytes 786440 | tf_op jit(solution)/shard_map/ppermute | solution.py:29
  971.3 33.6 %collective-permute-start.13 = (f32[256,256]{1,0:T(8,128)S(1)}, f32[256,256]{1,0:T(8,128)S(1)}, u32[]{:S(2)}, u32[]{:S(2)}) collective-permute-start(f32[256,256]{1,0:T(8,128)S(1)} %fusion.164), channel_id=1, source_target_pairs={{4,0},{5,1},{6,2},{7,3},{8,4},{9,5},{10,6},{11,7},{12,8},{13,9},{1... | collective-permute-start | bytes 786440 | tf_op jit(solution)/shard_map/ppermute | solution.py:29
  972.6 33.5 %collective-permute-start.12 = (f32[256,256]{1,0:T(8,128)S(1)}, f32[256,256]{1,0:T(8,128)S(1)}, u32[]{:S(2)}, u32[]{:S(2)}) collective-permute-start(f32[256,256]{1,0:T(8,128)S(1)} %fusion.164), channel_id=1, source_target_pairs={{5,0},{6,1},{7,2},{8,3},{9,4},{10,5},{11,6},{12,7},{13,8},{14,9},{... | collective-permute-start | bytes 786440 | tf_op jit(solution)/shard_map/ppermute | solution.py:29
  976.0 36.4 %collective-permute-start.11 = (f32[256,256]{1,0:T(8,128)S(1)}, f32[256,256]{1,0:T(8,128)S(1)}, u32[]{:S(2)}, u32[]{:S(2)}) collective-permute-start(f32[256,256]{1,0:T(8,128)S(1)} %fusion.164), channel_id=1, source_target_pairs={{6,0},{7,1},{8,2},{9,3},{10,4},{11,5},{12,6},{13,7},{14,8},{15,9},... | collective-permute-start | bytes 786440 | tf_op jit(solution)/shard_map/ppermute | solution.py:29
  986.0 27.9 %collective-permute-start.10 = (f32[256,256]{1,0:T(8,128)S(1)}, f32[256,256]{1,0:T(8,128)S(1)}, u32[]{:S(2)}, u32[]{:S(2)}) collective-permute-start(f32[256,256]{1,0:T(8,128)S(1)} %fusion.164), channel_id=1, source_target_pairs={{7,0},{8,1},{9,2},{10,3},{11,4},{12,5},{13,6},{14,7},{15,8},{23,16... | collective-permute-start | bytes 786440 | tf_op jit(solution)/shard_map/ppermute | solution.py:29
  989.4 76.8 %collective-permute-start.9 = (f32[256,256]{1,0:T(8,128)S(1)}, f32[256,256]{1,0:T(8,128)S(1)}, u32[]{:S(2)}, u32[]{:S(2)}) collective-permute-start(f32[256,256]{1,0:T(8,128)S(1)} %fusion.164), channel_id=1, source_target_pairs={{8,0},{9,1},{10,2},{11,3},{12,4},{13,5},{14,6},{15,7},{24,16},{25,... | collective-permute-start | bytes 786440 | tf_op jit(solution)/shard_map/ppermute | solution.py:29
  1004.9 66.5 %collective-permute-start.8 = (f32[256,256]{1,0:T(8,128)S(1)}, f32[256,256]{1,0:T(8,128)S(1)}, u32[]{:S(2)}, u32[]{:S(2)}) collective-permute-start(f32[256,256]{1,0:T(8,128)S(1)} %fusion.164), channel_id=1, source_target_pairs={{9,0},{10,1},{11,2},{12,3},{13,4},{14,5},{15,6},{25,16},{26,17},{2... | collective-permute-start | bytes 786440 | tf_op jit(solution)/shard_map/ppermute | solution.py:29
  1006.2 66.5 %collective-permute-start.7 = (f32[256,256]{1,0:T(8,128)S(1)}, f32[256,256]{1,0:T(8,128)S(1)}, u32[]{:S(2)}, u32[]{:S(2)}) collective-permute-start(f32[256,256]{1,0:T(8,128)S(1)} %fusion.164), channel_id=1, source_target_pairs={{10,0},{11,1},{12,2},{13,3},{14,4},{15,5},{26,16},{27,17},{28,18},... | collective-permute-start | bytes 786440 | tf_op jit(solution)/shard_map/ppermute | solution.py:29
  1012.5 82.4 %collective-permute-start.6 = (f32[256,256]{1,0:T(8,128)S(1)}, f32[256,256]{1,0:T(8,128)S(1)}, u32[]{:S(2)}, u32[]{:S(2)}) collective-permute-start(f32[256,256]{1,0:T(8,128)S(1)} %fusion.164), channel_id=1, source_target_pairs={{11,0},{12,1},{13,2},{14,3},{15,4},{27,16},{28,17},{29,18},{30,19}... | collective-permute-start | bytes 786440 | tf_op jit(solution)/shard_map/ppermute | solution.py:29
  1013.9 81.0 %collective-permute-start.5 = (f32[256,256]{1,0:T(8,128)S(1)}, f32[256,256]{1,0:T(8,128)S(1)}, u32[]{:S(2)}, u32[]{:S(2)}) collective-permute-start(f32[256,256]{1,0:T(8,128)S(1)} %fusion.164), channel_id=1, source_target_pairs={{12,0},{13,1},{14,2},{15,3},{28,16},{29,17},{30,18},{31,19}} | collective-permute-start | bytes 786440 | tf_op jit(solution)/shard_map/ppermute | solution.py:29
  1066.2 28.7 %collective-permute-start.4 = (f32[256,256]{1,0:T(8,128)S(1)}, f32[256,256]{1,0:T(8,128)S(1)}, u32[]{:S(2)}, u32[]{:S(2)}) collective-permute-start(f32[256,256]{1,0:T(8,128)S(1)} %fusion.164), channel_id=1, source_target_pairs={{13,0},{14,1},{15,2},{29,16},{30,17},{31,18}} | collective-permute-start | bytes 786440 | tf_op jit(solution)/shard_map/ppermute | solution.py:29
  1071.4 23.5 %collective-permute-start.3 = (f32[256,256]{1,0:T(8,128)S(1)}, f32[256,256]{1,0:T(8,128)S(1)}, u32[]{:S(2)}, u32[]{:S(2)}) collective-permute-start(f32[256,256]{1,0:T(8,128)S(1)} %fusion.164), channel_id=1, source_target_pairs={{14,0},{15,1},{30,16},{31,17}} | collective-permute-start | bytes 786440 | tf_op jit(solution)/shard_map/ppermute | solution.py:29
  1072.7 22.2 %collective-permute-start.2 = (f32[256,256]{1,0:T(8,128)S(1)}, f32[256,256]{1,0:T(8,128)S(1)}, u32[]{:S(2)}, u32[]{:S(2)}) collective-permute-start(f32[256,256]{1,0:T(8,128)S(1)} %fusion.164), channel_id=1, source_target_pairs={{15,0},{31,16}} | collective-permute-start | bytes 786440 | tf_op jit(solution)/shard_map/ppermute | solution.py:29
Sparse Core Ops, SparseCore 0:
  785.7 75.0 reduce-scatter.1
where the time goes:
time: 1110 us; the launch traced here: 1100 us
  other arithmetic  634 us (57%)
  waiting for transfers between devices  162 us (15%)
  local copies, waits for them, and re-layouts  121 us (11%)
  starting transfers between devices  79.8 us (7%)
  between operations  75 us (7%)
  matrix products  19.8 us (2%)
  loops' own time  11.3 us (1%)
    convert_element_type x32, other arithmetic, tap_matrix(): return (real_part.astype(jnp.bfloat16), imag_part.astype(jnp.bfloat16))  561 us
    ppermute x30, waiting for transfers between devices, passed_along(): return lax.ppermute(block, axis, route)  109 us
    ppermute x30, starting transfers between devices, passed_along(): return lax.ppermute(block, axis, route)  75.5 us
    gather x32, local copies, waits for them, and re-layouts, tap_matrix(): amplitude = jnp.take(pupil_taps, clipped) / math.sqrt(tap_count)  66.4 us
    reduce_scatter x1, waiting for transfers between devices, on_device(): lax.psum_scatter(partial_sum, 'src', scatter_dimension=0, tiled=True)  53 us
    dynamic_update_slice x16, other arithmetic, on_device(): lax.map(plane_term, focus_steps).reshape(planes * rows_tile, cols_tile)  33.5 us
    neg x16, other arithmetic, field_power(): lower_half = jnp.concatenate([-cols_imag.T, cols_real.T], axis=1)  32.3 us
    slice x16, local copies, waits for them, and re-layouts, plane_term(): running = running + factors[source] * power  27.3 us
  transfers between devices with their start and end apart: 33, of which 15 were waited for; matrix products, arithmetic and copies ran while one was open for 0% of the time, Pallas kernels for 0%

commit v1 on v0

--- a/solution.py
+++ b/solution.py
@@ -3,6 +3,8 @@
 import jax
 import jax.numpy as jnp
 from jax import lax
+from jax.experimental import pallas as pl
+from jax.experimental.pallas import tpu as pltpu
 from jax.sharding import PartitionSpec as P
 
 two_pi = 2.0 * math.pi
@@ -115,9 +117,179 @@
     return (intensity, latent)
 
 
+max_shift = 8
+shifts = 2 * max_shift + 1
+lanes = 512
+
+
+def exact_dot(left, right):
+    return jnp.dot(left, right, precision=lax.Precision.HIGHEST, preferred_element_type=jnp.float32)
+
+
+def store_toeplitz(row, position, pieces):
+    base = pltpu.roll(jnp.broadcast_to(row, (16, lanes)), position, 1, stride=1, stride_axis=0)
+    for j in range(8):
+        rolled = pltpu.roll(base, lanes - 128 + 16 * j, 1)
+        for block, start in ((j + 8, 0), (j, 128)):
+            part = rolled[:, start : start + 256]
+            for ref, top, side, sign in pieces:
+                value = part if sign > 0 else -part
+                ref[top + 16 * block : top + 16 * block + 16, side : side + 256] = value.astype(
+                    ref.dtype
+                )
+
+
+def store_taps(taps_ref, row, focus, flip, real_ref, imag_ref, tap_count):
+    centre = (tap_count - 1) / 2.0
+    amplitude = taps_ref[row : row + 1, :128] / math.sqrt(tap_count)
+    shape = (24, 128)
+    relative = (lax.broadcasted_iota(jnp.int32, shape, 1).astype(jnp.float32) - centre) * flip
+    tilt = (lax.broadcasted_iota(jnp.int32, shape, 0) - max_shift).astype(jnp.float32)
+    phase = (
+        two_pi * tilt * relative / tap_count + defocus_scale * focus * (relative / centre) ** 2
+    )
+    real_ref[...] = jnp.zeros_like(real_ref)
+    imag_ref[...] = jnp.zeros_like(imag_ref)
+    real_ref[:, :128] = amplitude * jnp.cos(phase)
+    imag_ref[:, :128] = amplitude * jnp.sin(phase)
+
+
+def build_tables(tap_count, mask_ref, rows_ref, focus, tap_refs, stacked, fields, pupils):
+    forward_real, forward_imag, back_real, back_imag = tap_refs
+    store_taps(rows_ref, 0, focus, 1.0, forward_real, forward_imag, tap_count)
+    store_taps(rows_ref, 1, focus, -1.0, back_real, back_imag, tap_count)
+    mask_bf = mask_ref[...].astype(jnp.float32).astype(jnp.bfloat16)
+
+    def one_shift(shift, carry):
+        row = pl.ds(shift, 1)
+        store_toeplitz(forward_real[row, :], 232, ((stacked, 0, 0, 1),))
+        store_toeplitz(forward_imag[row, :], 232, ((stacked, 256, 0, 1),))
+        first = jnp.dot(stacked[...], mask_bf, preferred_element_type=jnp.float32)
+        fields[shift, :, :256] = first[:256].astype(jnp.bfloat16)
+        fields[shift, :, 256:] = first[256:].astype(jnp.bfloat16)
+        pupil = pupils.at[shift]
+        store_toeplitz(back_real[row, :], 233, ((pupil, 0, 0, 1), (pupil, 256, 256, 1)))
+        store_toeplitz(back_imag[row, :], 233, ((pupil, 0, 256, 1), (pupil, 256, 0, -1)))
+        return carry
+
+    lax.fori_loop(0, shifts, one_shift, 0)
+
+
+def image_kernel(
+    tap_count, points_ref, focus_ref, mask_ref, rows_ref, intensity_ref, along_ref,
+    t0, t1, t2, t3, stacked, fields, pupils, blur,
+):
+    me = lax.axis_index("src")
+    total = points_ref.shape[0]
+    focus = focus_ref[me].astype(jnp.float32)
+    build_tables(tap_count, mask_ref, rows_ref, focus, (t0, t1, t2, t3), stacked, fields, pupils)
+    store_toeplitz(rows_ref[2:3, :], 241, ((blur, 0, 0, 1),))
+    intensity_ref[...] = jnp.zeros_like(intensity_ref)
+
+    def one_source(s, carry):
+        factor = points_ref[s, 2].astype(jnp.float32) / (4.0 * total)
+        field = jnp.dot(
+            fields[points_ref[s, 1] + max_shift],
+            pupils[points_ref[s, 0] + max_shift],
+            preferred_element_type=jnp.float32,
+        )
+        intensity_ref[...] += factor * (field[:, :256] ** 2 + field[:, 256:] ** 2)
+        return carry
+
+    lax.fori_loop(0, total, one_source, 0)
+    acid = 1.0 - jnp.exp(-dose_scale * intensity_ref[...])
+    along_ref[...] = exact_dot(blur[...], acid.T)
+
+
+def stack_blur(stack, rows_ref, blur_z_ref, centre, planes, wide):
+    back_y = rows_ref[3:4, :]
+    store_toeplitz(back_y, 241, ((centre, 0, 0, 1),))
+    tall = jnp.broadcast_to(back_y, (16, lanes))
+    before = pltpu.roll(tall, lanes - 31, 1, stride=1, stride_axis=0)[:, :256]
+    after = pltpu.roll(tall, 241, 1, stride=1, stride_axis=0)[:, :256]
+    pad = jnp.zeros((240, 256), jnp.float32)
+    zero = jnp.zeros((wide, 256), jnp.float32)
+    along_y = (
+        exact_dot(stack, centre[...])
+        + exact_dot(
+            jnp.concatenate([zero, stack[:-wide]], axis=0), jnp.concatenate([pad, before], axis=0)
+        )
+        + exact_dot(
+            jnp.concatenate([stack[wide:], zero], axis=0), jnp.concatenate([after, pad], axis=0)
+        )
+    )
+    distance = lax.broadcasted_iota(jnp.int32, (256, 256), 0) - lax.broadcasted_iota(
+        jnp.int32, (256, 256), 1
+    )
+    mix = jnp.zeros((256, 256), jnp.float32)
+    for lag in range(1 - planes, planes):
+        mix = jnp.where(distance == lag * wide, blur_z_ref[lag + planes - 1] / planes, mix)
+    return exact_dot(mix, along_y)
+
+
+def stack_kernel(planes, wide, blur_z_ref, stack_ref, rows_ref, out_ref, centre):
+    out_ref[...] = stack_blur(stack_ref[...], rows_ref, blur_z_ref, centre, planes, wide)
+
+
+def padded_rows(pupil_taps, blur_x, blur_y):
+    parts = (
+        pupil_taps,
+        pupil_taps[::-1],
+        blur_x / blur_x.shape[0],
+        (blur_y / blur_y.shape[0])[::-1],
+    )
+    rows = [jnp.pad(part, (0, lanes - part.shape[0])) for part in parts]
+    return jnp.concatenate([jnp.stack(rows), jnp.zeros((4, lanes), jnp.float32)], axis=0)
+
+
+vmem = pl.BlockSpec(memory_space=pltpu.VMEM)
+smem = pl.BlockSpec(memory_space=pltpu.SMEM)
+
+
+def table_scratch():
+    return [pltpu.VMEM((24, lanes), jnp.float32)] * 4 + [
+        pltpu.VMEM((512, 256), jnp.bfloat16),
+        pltpu.VMEM((shifts, 256, 512), jnp.bfloat16),
+        pltpu.VMEM((shifts, 512, 512), jnp.bfloat16),
+        pltpu.VMEM((256, 256), jnp.float32),
+    ]
+
+
+def plane_per_device(
+    layout_mask, source_coords, source_weights, focus_steps, pupil_taps, blur_x, blur_y, blur_z
+):
+    devices = lax.axis_size("src")
+    wide = layout_mask.shape[1] // devices
+    local = jnp.concatenate([source_coords, source_weights[:, None]], axis=1)
+    points = lax.all_gather(local, "src", axis=0, tiled=True)
+    rows = padded_rows(pupil_taps, blur_x, blur_y)
+    square = jax.ShapeDtypeStruct((256, 256), jnp.float32)
+    limit = pltpu.CompilerParams(vmem_limit_bytes=48 * 2**20)
+    intensity, along = pl.pallas_call(
+        lambda *refs: image_kernel(pupil_taps.shape[0], *refs),
+        out_shape=(square, square),
+        in_specs=[smem, smem, vmem, vmem],
+        out_specs=(vmem, vmem),
+        scratch_shapes=table_scratch(),
+        compiler_params=limit,
+    )(points, focus_steps, layout_mask, rows)
+    stack = lax.all_to_all(along, "src", 0, 0, tiled=True)
+    mixed = pl.pallas_call(
+        lambda *refs: stack_kernel(devices, wide, *refs),
+        out_shape=square,
+        in_specs=[smem, vmem, vmem],
+        out_specs=vmem,
+        scratch_shapes=[pltpu.VMEM((256, 256), jnp.float32)],
+        compiler_params=limit,
+    )(blur_z, stack, rows)
+    latent = lax.all_to_all(mixed, "src", 0, 0, tiled=True).T
+    return intensity, latent
+
+
 def solution(mesh):
     in_specs = (P("groups", None), P("src", None), P("src"), P(), P(), P(), P(), P())
     out_specs = (P(("groups", "src"), None), P(("groups", "src"), None))
+    body = plane_per_device if mesh.shape["src"] == 16 else on_device
     return jax.shard_map(
-        on_device, mesh=mesh, in_specs=in_specs, out_specs=out_specs, check_vma=False
-    )
+        body, mesh=mesh, in_specs=in_specs, out_specs=out_specs, check_vma=False
+    )

time: 1110 us -> 77.2 us (0.07)
  other arithmetic: 634 us -> 0.74 us
  waiting for transfers between devices: 162 us -> 0 us
  local copies, waits for them, and re-layouts: 121 us -> 5.39 us
  starting transfers between devices: 79.8 us -> 0 us
  between operations: 75 us -> 0.69 us
  blocking collectives: 0 us -> 48.5 us
  Pallas kernels: 0 us -> 21.5 us
  matrix products: 19.8 us -> 0 us
  loops' own time: 11.3 us -> 0 us
    convert_element_type x33 -> x0, other arithmetic: 562 us -> none  [the longest x32 561 us: tap_matrix(): return (real_part.astype(jnp.bfloat16), imag_part.astype(jnp.bfloat16))]
    ppermute x32 -> x0, waiting for transfers between devices: 109 us -> none  [the longest x30 109 us: passed_along(): return lax.ppermute(block, axis, route)]
    ppermute x32 -> x0, starting transfers between devices: 79.8 us -> none  [the longest x30 75.5 us: passed_along(): return lax.ppermute(block, axis, route)]
    gather x32 -> x0, local copies, waits for them, and re-layouts: 66.4 us -> none  [tap_matrix(): amplitude = jnp.take(pupil_taps, clipped) / math.sqrt(tap_count)]
    reduce_scatter x1 -> x0, waiting for transfers between devices: 53 us -> none  [on_device(): lax.psum_scatter(partial_sum, 'src', scatter_dimension=0, tiled=True)]
    slice x56 -> x0, local copies, waits for them, and re-layouts: 33.7 us -> none  [the longest x16 27.3 us: plane_term(): running = running + factors[source] * power]
    dynamic_update_slice x16 -> x0, other arithmetic: 33.5 us -> none  [on_device(): lax.map(plane_term, focus_steps).reshape(planes * rows_tile, cols_tile)]
    neg x16 -> x0, other arithmetic: 32.3 us -> none  [field_power(): lower_half = jnp.concatenate([-cols_imag.T, cols_real.T], axis=1)]
  transfers between devices with their start and end apart: 33 -> 0, of which waited for: 15 -> 0; matrix products, arithmetic and copies ran while one was open for 0% -> 0% of each run, Pallas kernels for 0% -> 0%
where the time goes in v1:
time: 77.2 us; the launch traced here: 76.9 us
  blocking collectives  48.5 us (63%)
  Pallas kernels  21.5 us (28%)
  local copies, waits for them, and re-layouts  5.39 us (7%)
    all_gather x1, blocking collectives, plane_per_device(): points = lax.all_gather(local, 'src', axis=0, tiled=True)  23.1 us
    pallas_call x1, Pallas kernels, plane_per_device(): pl.pallas_call(lambda *refs: image_kernel(pupil_taps.shape[0], *refs), ou...  19.2 us
    all_to_all x1, blocking collectives, plane_per_device(): latent = lax.all_to_all(mixed, 'src', 0, 0, tiled=True).T  12.8 us
    all_to_all x1, blocking collectives, plane_per_device(): stack = lax.all_to_all(along, 'src', 0, 0, tiled=True)  12.6 us
    unnamed x15, local copies, waits for them, and re-layouts  5.06 us
    pallas_call x1, Pallas kernels, plane_per_device(): pl.pallas_call(lambda *refs: stack_kernel(devices, wide, *refs), out_shap...  2.32 us

profile of v1, /device:TPU:0, one launch (start us, length us, event | category | flops | bytes accessed | tf_op | source)
XLA Modules:
  0.0 76.9 jit_solution(2687509166074053108)
XLA Ops:
  0.6 0.0 copy-start.5
  0.6 0.7 broadcast_multiply_fusion.1
  1.3 0.0 copy-done.5
  1.3 0.1 reverse.3
  1.4 0.0 copy-start.4
  1.4 0.6 copy-done.4
  2.1 0.1 rev.6
  2.2 0.0 copy-start.6
  2.2 0.7 copy-done.6
  2.8 0.1 copy.18
  2.9 0.0 copy-start.3
  2.9 0.7 copy-done.3
  3.6 0.1 add_bitcast_fusion
  3.7 23.1 %all-gather = s32[16,2,3]{2,1,0:T(2,128)S(1)} all-gather(s32[1,2,3]{2,1,0:T(2,128)S(1)} %add_bitcast_fusion), channel_id=1, replica_groups=mesh['groups'=2,'src'=16] {'src'}, dimensions={0}, use_global_device_ids=true | all-gather | bytes 408 | tf_op jit(solution)/shard_map/all_gather | solution.py:264
  26.8 0.0 copy-start.1
  26.8 0.6 copy-done.1
  27.5 0.0 copy-start
  27.5 0.9 %copy-done = s32[256,256]{1,0:T(8,128)S(1)} copy-done((s32[256,256]{1,0:T(8,128)S(1)}, s32[256,256]{1,0:T(8,128)}, u32[]{:S(2)}) %copy-start) | copy-done | bytes 262168
  28.4 19.2 %shard_map.95 = (f32[256,256]{1,0:T(8,128)}, f32[256,256]{1,0:T(8,128)S(1)}) custom-call(s32[32,3]{1,0:T(8,128)S(1)} %bitcast.17, s32[16]{0:T(128)S(1)} %copy-done.1, s32[256,256]{1,0:T(8,128)S(1)} %copy-done, f32[8,512]{1,0:T(8,128)S(1)} %concatenate.7.refs_3_.refs_2_), custom_call_target="tpu_custom_call" | custom-call | tf_op jit(solution)/shard_map/pallas_call | solution.py:268
  47.6 12.6 %all_to_all.23 = f32[16,16,256]{2,1,0:T(8,128)S(1)} all-to-all(f32[16,16,256]{2,1,0:T(8,128)S(1)} %bitcast.16), channel_id=1, replica_groups=mesh['groups'=2,'src'=16] {'src'}, dimensions={0} | all-to-all | bytes 524288 | tf_op jit(solution)/shard_map/all_to_all | solution.py:276
  60.2 0.0 copy-start.2
  60.2 0.7 copy-done.2
  60.9 2.3 %shard_map.96 = f32[256,256]{1,0:T(8,128)S(1)} custom-call(f32[31]{0:T(128)S(1)} %copy-done.2, f32[256,256]{1,0:T(8,128)S(1)} %bitcast.14, f32[8,512]{1,0:T(8,128)S(1)} %concatenate.7.refs_3_.refs_2_), custom_call_target="tpu_custom_call" | custom-call | tf_op jit(solution)/shard_map/pallas_call | solution.py:277
  63.2 12.8 %all_to_all.24 = f32[16,16,256]{2,1,0:T(8,128)S(1)} all-to-all(f32[16,16,256]{2,1,0:T(8,128)S(1)} %bitcast.15), channel_id=1, replica_groups=mesh['groups'=2,'src'=16] {'src'}, dimensions={0} | all-to-all | bytes 524288 | tf_op jit(solution)/shard_map/all_to_all | solution.py:285
  76.0 0.8 %copy.21 = f32[256,256]{1,0:T(8,128)} copy(f32[256,256]{0,1:T(8,128)S(1)} %bitcast.18) | data formatting | bytes 524288
  (7 shorter events, 0.1 us)
Async XLA Ops:
  0.6 0.7 copy-start.5
  1.4 0.7 copy-start.4
  2.2 0.7 copy-start.6
  2.9 0.7 copy-start.3
  26.8 0.7 copy-start.1
  27.5 0.9 %copy-start = (s32[256,256]{1,0:T(8,128)S(1)}, s32[256,256]{1,0:T(8,128)}, u32[]{:S(2)}) copy-start(s32[256,256]{1,0:T(8,128)} %refs_2_.1) | copy-start | bytes 786436
  60.2 0.7 copy-start.2

commit v2 on v1

--- a/solution.py
+++ b/solution.py
@@ -175,39 +175,120 @@
     lax.fori_loop(0, shifts, one_shift, 0)
 
 
-def image_kernel(
-    tap_count, points_ref, focus_ref, mask_ref, rows_ref, intensity_ref, along_ref,
-    t0, t1, t2, t3, stacked, fields, pupils, blur,
+def lane_row(count, value):
+    lane = lax.broadcasted_iota(jnp.int32, (1, lanes), 1)
+    row = jnp.zeros((1, lanes), jnp.float32)
+    for t in range(count):
+        row = jnp.where(lane == t, value(t), row)
+    return row
+
+
+def plane_kernel(
+    n, wide, mask_ref, coords_ref, weights_ref, focus_ref, taps_ref, blur_x_ref, blur_y_ref,
+    blur_z_ref, intensity_ref, latent_ref, rows, t0, t1, t2, t3, stacked, fields, pupils, blur,
+    centre, mix, own, points, points_smem, along, columns, mixed, planes, send_sems, recv_sems,
+    local_sem,
 ):
     me = lax.axis_index("src")
-    total = points_ref.shape[0]
+    group = lax.axis_index("groups")
+    local = weights_ref.shape[0]
+    tap_count, blur_count = taps_ref.shape[0], blur_x_ref.shape[0]
+    barrier = pltpu.get_barrier_semaphore()
+
+    def each(action):
+        lax.fori_loop(1, n, lambda off, carry: (action(off), carry)[1], 0)
+
+    def peer(off):
+        return (group, lax.rem(me + off, n))
+
+    def signal(off):
+        pl.semaphore_signal(
+            barrier, inc=1, device_id=peer(off), device_id_type=pl.DeviceIdType.MESH
+        )
+
+    def copy(phase, source, target, off, slot):
+        return pltpu.make_async_remote_copy(
+            src_ref=source(off),
+            dst_ref=target.at[slot],
+            send_sem=send_sems.at[phase, off],
+            recv_sem=recv_sems.at[phase, off],
+            device_id=peer(off),
+            device_id_type=pl.DeviceIdType.MESH,
+        )
+
+    def start(phase, source, target):
+        each(lambda off: copy(phase, source, target, off, me).start())
+
+    def receive(phase, source, target):
+        each(
+            lambda off: copy(
+                phase, source, target, off, lax.rem(me + n - off, n)
+            ).wait_recv()
+        )
+
+    def sent(phase, source, target):
+        each(lambda off: copy(phase, source, target, off, me).wait_send())
+
+    each(signal)
+    lane = lax.broadcasted_iota(jnp.int32, (1, 128), 1)
+    packed = jnp.zeros((1, 128), jnp.int32)
+    for s in range(local):
+        packed = jnp.where(lane == 3 * s, coords_ref[s, 0], packed)
+        packed = jnp.where(lane == 3 * s + 1, coords_ref[s, 1], packed)
+        packed = jnp.where(lane == 3 * s + 2, weights_ref[s], packed)
+    own[...] = packed
+    points[me] = packed
+    rows[0:1, :] = lane_row(tap_count, lambda t: taps_ref[t])
+    rows[1:2, :] = lane_row(tap_count, lambda t: taps_ref[tap_count - 1 - t])
+    rows[2:3, :] = lane_row(blur_count, lambda t: blur_x_ref[t] / blur_count)
+    rows[3:4, :] = lane_row(blur_count, lambda t: blur_y_ref[blur_count - 1 - t] / blur_count)
+    pl.semaphore_wait(barrier, n - 1)
+    point_source = lambda off: own
+    start(0, point_source, points)
+
     focus = focus_ref[me].astype(jnp.float32)
-    build_tables(tap_count, mask_ref, rows_ref, focus, (t0, t1, t2, t3), stacked, fields, pupils)
-    store_toeplitz(rows_ref[2:3, :], 241, ((blur, 0, 0, 1),))
+    build_tables(tap_count, mask_ref, rows, focus, (t0, t1, t2, t3), stacked, fields, pupils)
+    store_toeplitz(rows[2:3, :], 241, ((blur, 0, 0, 1),))
     intensity_ref[...] = jnp.zeros_like(intensity_ref)
-
-    def one_source(s, carry):
-        factor = points_ref[s, 2].astype(jnp.float32) / (4.0 * total)
-        field = jnp.dot(
-            fields[points_ref[s, 1] + max_shift],
-            pupils[points_ref[s, 0] + max_shift],
-            preferred_element_type=jnp.float32,
-        )
-        intensity_ref[...] += factor * (field[:, :256] ** 2 + field[:, 256:] ** 2)
+    receive(0, point_source, points)
+    to_smem = pltpu.make_async_copy(points, points_smem, local_sem)
+    to_smem.start()
+    to_smem.wait()
+
+    def one_device(device, carry):
+        for s in range(local):
+            point = [points_smem[device, 0, 3 * s + item] for item in range(3)]
+            factor = point[2].astype(jnp.float32) / (4.0 * local * n)
+            field = jnp.dot(
+                fields[point[1] + max_shift],
+                pupils[point[0] + max_shift],
+                preferred_element_type=jnp.float32,
+            )
+            intensity_ref[...] += factor * (field[:, :256] ** 2 + field[:, 256:] ** 2)
         return carry
 
-    lax.fori_loop(0, total, one_source, 0)
+    lax.fori_loop(0, n, one_device, 0)
     acid = 1.0 - jnp.exp(-dose_scale * intensity_ref[...])
-    along_ref[...] = exact_dot(blur[...], acid.T)
-
-
-def stack_blur(stack, rows_ref, blur_z_ref, centre, planes, wide):
-    back_y = rows_ref[3:4, :]
+    along[...] = exact_dot(blur[...], acid.T).reshape(n, wide, 256)
+    column_source = lambda off: along.at[lax.rem(me + off, n)]
+    start(1, column_source, columns)
+    columns[me] = along[me]
+
+    back_y = rows[3:4, :]
     store_toeplitz(back_y, 241, ((centre, 0, 0, 1),))
     tall = jnp.broadcast_to(back_y, (16, lanes))
     before = pltpu.roll(tall, lanes - 31, 1, stride=1, stride_axis=0)[:, :256]
     after = pltpu.roll(tall, 241, 1, stride=1, stride_axis=0)[:, :256]
     pad = jnp.zeros((240, 256), jnp.float32)
+    distance = lax.broadcasted_iota(jnp.int32, (256, 256), 0) - lax.broadcasted_iota(
+        jnp.int32, (256, 256), 1
+    )
+    mix[...] = jnp.zeros_like(mix)
+    for lag in range(1 - n, n):
+        mix[...] = jnp.where(distance == lag * wide, blur_z_ref[lag + n - 1] / n, mix[...])
+
+    receive(1, column_source, columns)
+    stack = columns[...].reshape(256, 256)
     zero = jnp.zeros((wide, 256), jnp.float32)
     along_y = (
         exact_dot(stack, centre[...])
@@ -218,72 +299,58 @@
             jnp.concatenate([stack[wide:], zero], axis=0), jnp.concatenate([after, pad], axis=0)
         )
     )
-    distance = lax.broadcasted_iota(jnp.int32, (256, 256), 0) - lax.broadcasted_iota(
-        jnp.int32, (256, 256), 1
-    )
-    mix = jnp.zeros((256, 256), jnp.float32)
-    for lag in range(1 - planes, planes):
-        mix = jnp.where(distance == lag * wide, blur_z_ref[lag + planes - 1] / planes, mix)
-    return exact_dot(mix, along_y)
-
-
-def stack_kernel(planes, wide, blur_z_ref, stack_ref, rows_ref, out_ref, centre):
-    out_ref[...] = stack_blur(stack_ref[...], rows_ref, blur_z_ref, centre, planes, wide)
-
-
-def padded_rows(pupil_taps, blur_x, blur_y):
-    parts = (
-        pupil_taps,
-        pupil_taps[::-1],
-        blur_x / blur_x.shape[0],
-        (blur_y / blur_y.shape[0])[::-1],
-    )
-    rows = [jnp.pad(part, (0, lanes - part.shape[0])) for part in parts]
-    return jnp.concatenate([jnp.stack(rows), jnp.zeros((4, lanes), jnp.float32)], axis=0)
-
-
-vmem = pl.BlockSpec(memory_space=pltpu.VMEM)
-smem = pl.BlockSpec(memory_space=pltpu.SMEM)
-
-
-def table_scratch():
-    return [pltpu.VMEM((24, lanes), jnp.float32)] * 4 + [
-        pltpu.VMEM((512, 256), jnp.bfloat16),
-        pltpu.VMEM((shifts, 256, 512), jnp.bfloat16),
-        pltpu.VMEM((shifts, 512, 512), jnp.bfloat16),
-        pltpu.VMEM((256, 256), jnp.float32),
-    ]
+    mixed[...] = exact_dot(mix[...], along_y).reshape(n, wide, 256)
+    plane_source = lambda off: mixed.at[lax.rem(me + off, n)]
+    start(2, plane_source, planes)
+    planes[me] = mixed[me]
+    sent(0, point_source, points)
+    sent(1, column_source, columns)
+    receive(2, plane_source, planes)
+    latent_ref[...] = planes[...].reshape(256, 256).T
+    sent(2, plane_source, planes)
 
 
 def plane_per_device(
     layout_mask, source_coords, source_weights, focus_steps, pupil_taps, blur_x, blur_y, blur_z
 ):
-    devices = lax.axis_size("src")
-    wide = layout_mask.shape[1] // devices
-    local = jnp.concatenate([source_coords, source_weights[:, None]], axis=1)
-    points = lax.all_gather(local, "src", axis=0, tiled=True)
-    rows = padded_rows(pupil_taps, blur_x, blur_y)
+    n = lax.axis_size("src")
+    wide = layout_mask.shape[1] // n
     square = jax.ShapeDtypeStruct((256, 256), jnp.float32)
-    limit = pltpu.CompilerParams(vmem_limit_bytes=48 * 2**20)
-    intensity, along = pl.pallas_call(
-        lambda *refs: image_kernel(pupil_taps.shape[0], *refs),
+    full = pltpu.VMEM((256, 256), jnp.float32)
+    parts = pltpu.VMEM((n, wide, 256), jnp.float32)
+    vmem = pl.BlockSpec(memory_space=pltpu.VMEM)
+    smem = pl.BlockSpec(memory_space=pltpu.SMEM)
+    return pl.pallas_call(
+        lambda *refs: plane_kernel(n, wide, *refs),
         out_shape=(square, square),
-        in_specs=[smem, smem, vmem, vmem],
+        in_specs=[vmem] + [smem] * 7,
         out_specs=(vmem, vmem),
-        scratch_shapes=table_scratch(),
-        compiler_params=limit,
-    )(points, focus_steps, layout_mask, rows)
-    stack = lax.all_to_all(along, "src", 0, 0, tiled=True)
-    mixed = pl.pallas_call(
-        lambda *refs: stack_kernel(devices, wide, *refs),
-        out_shape=square,
-        in_specs=[smem, vmem, vmem],
-        out_specs=vmem,
-        scratch_shapes=[pltpu.VMEM((256, 256), jnp.float32)],
-        compiler_params=limit,
-    )(blur_z, stack, rows)
-    latent = lax.all_to_all(mixed, "src", 0, 0, tiled=True).T
-    return intensity, latent
+        scratch_shapes=[pltpu.VMEM((8, lanes), jnp.float32)]
+        + [pltpu.VMEM((24, lanes), jnp.float32)] * 4
+        + [
+            pltpu.VMEM((512, 256), jnp.bfloat16),
+            pltpu.VMEM((shifts, 256, 512), jnp.bfloat16),
+            pltpu.VMEM((shifts, 512, 512), jnp.bfloat16),
+            full,
+            full,
+            full,
+            pltpu.VMEM((1, 128), jnp.int32),
+            pltpu.VMEM((n, 1, 128), jnp.int32),
+            pltpu.SMEM((n, 1, 128), jnp.int32),
+            parts,
+            parts,
+            parts,
+            parts,
+            pltpu.SemaphoreType.DMA((3, n)),
+            pltpu.SemaphoreType.DMA((3, n)),
+            pltpu.SemaphoreType.DMA,
+        ],
+        compiler_params=pltpu.CompilerParams(
+            vmem_limit_bytes=48 * 2**20, collective_id=0, has_side_effects=True
+        ),
+    )(
+        layout_mask, source_coords, source_weights, focus_steps, pupil_taps, blur_x, blur_y, blur_z
+    )
 
 
 def solution(mesh):

time: 77.2 us -> 46.1 us (0.60)
  blocking collectives: 48.5 us -> 0 us
  Pallas kernels: 21.5 us -> 38.3 us
  local copies, waits for them, and re-layouts: 5.39 us -> 6.96 us
    all_to_all x2 -> x0, blocking collectives: 25.5 us -> none  [the longest x1 12.8 us: plane_per_device(): latent = lax.all_to_all(mixed, 'src', 0, 0, tiled=True).T]
    all_gather x1 -> x0, blocking collectives: 23.1 us -> none  [plane_per_device(): points = lax.all_gather(local, 'src', axis=0, tiled=True)]
    pallas_call x2 -> x1, Pallas kernels: 21.5 us -> 38.3 us  [plane_per_device(): pl.pallas_call(lambda *refs: plane_kernel(n, wide, *refs), out_shape=(squ...]
    unnamed x15 -> x18, local copies, waits for them, and re-layouts: 5.06 us -> 6.96 us
where the time goes in v2:
time: 46.1 us; the launch traced here: 45.9 us
  Pallas kernels  38.3 us (83%)
  local copies, waits for them, and re-layouts  6.96 us (15%)
  between operations  0.66 us (1%)
    pallas_call x1, Pallas kernels, plane_per_device(): pl.pallas_call(lambda *refs: plane_kernel(n, wide, *refs), out_shape=(squ...  38.3 us
    unnamed x18, local copies, waits for them, and re-layouts  6.96 us

profile of v2, /device:TPU:0, one launch (start us, length us, event | category | flops | bytes accessed | tf_op | source)
XLA Modules:
  0.0 45.9 jit_solution(11239001021062787946)
XLA Ops:
  0.6 0.0 copy-start
  0.6 0.9 %copy-done = s32[256,256]{1,0:T(8,128)S(1)} copy-done((s32[256,256]{1,0:T(8,128)S(1)}, s32[256,256]{1,0:T(8,128)}, u32[]{:S(2)}) %copy-start) | copy-done | bytes 262168
  1.6 0.0 copy-start.1
  1.6 0.7 %copy-done.1 = s32[2,2]{1,0:T(2,128)S(1)} copy-done((s32[2,2]{1,0:T(2,128)S(1)}, s32[2,2]{1,0:T(2,128)}, u32[]{:S(2)}) %copy-start.1) | copy-done | bytes 40
  2.3 0.0 copy-start.2
  2.3 0.7 %copy-done.2 = s32[2]{0:T(128)S(1)} copy-done((s32[2]{0:T(128)S(1)}, s32[2]{0:T(128)}, u32[]{:S(2)}) %copy-start.2) | copy-done | bytes 32
  2.9 0.0 copy-start.3
  2.9 0.7 %copy-done.3 = s32[16]{0:T(128)S(1)} copy-done((s32[16]{0:T(128)S(1)}, s32[16]{0:T(128)}, u32[]{:S(2)}) %copy-start.3) | copy-done | bytes 88
  3.6 0.0 copy-start.4
  3.6 0.7 %copy-done.4 = f32[48]{0:T(128)S(1)} copy-done((f32[48]{0:T(128)S(1)}, f32[48]{0:T(128)}, u32[]{:S(2)}) %copy-start.4) | copy-done | bytes 216
  4.2 0.0 copy-start.5
  4.2 0.7 %copy-done.5 = f32[31]{0:T(128)S(1)} copy-done((f32[31]{0:T(128)S(1)}, f32[31]{0:T(128)}, u32[]{:S(2)}) %copy-start.5) | copy-done | bytes 148
  4.9 0.0 copy-start.6
  4.9 0.7 %copy-done.6 = f32[31]{0:T(128)S(1)} copy-done((f32[31]{0:T(128)S(1)}, f32[31]{0:T(128)}, u32[]{:S(2)}) %copy-start.6) | copy-done | bytes 148
  5.5 0.0 copy-start.7
  5.5 0.7 %copy-done.7 = f32[31]{0:T(128)S(1)} copy-done((f32[31]{0:T(128)S(1)}, f32[31]{0:T(128)}, u32[]{:S(2)}) %copy-start.7) | copy-done | bytes 148
  6.2 38.3 %shard_map.95 = (f32[256,256]{1,0:T(8,128)S(1)}, f32[256,256]{1,0:T(8,128)S(1)}) custom-call(s32[256,256]{1,0:T(8,128)S(1)} %copy-done, s32[2,2]{1,0:T(2,128)S(1)} %copy-done.1, s32[2]{0:T(128)S(1)} %copy-done.2, s32[16]{0:T(128)S(1)} %copy-done.3, f32[48]{0:T(128)S(1)} %copy-done.4, f32[31]{0:T(128)S(1)} %copy-done.5, f32[31]{0:T(128)S(1)} %copy-done.6, ...), custom_call_target="tpu_custom_call" | custom-call | tf_op jit(solution)/shard_map/pallas_call | solution.py:323
  44.5 0.7 %copy.12 = f32[256,256]{1,0:T(8,128)} copy(f32[256,256]{1,0:T(8,128)S(1)} %get-tuple-element.4) | data formatting | bytes 524288
  45.2 0.7 %copy.13 = f32[256,256]{1,0:T(8,128)} copy(f32[256,256]{1,0:T(8,128)S(1)} %get-tuple-element.5) | data formatting | bytes 524288
Async XLA Ops:
  0.6 1.0 %copy-start = (s32[256,256]{1,0:T(8,128)S(1)}, s32[256,256]{1,0:T(8,128)}, u32[]{:S(2)}) copy-start(s32[256,256]{1,0:T(8,128)} %refs_0_.1) | copy-start | bytes 786436
  1.6 0.7 %copy-start.1 = (s32[2,2]{1,0:T(2,128)S(1)}, s32[2,2]{1,0:T(2,128)}, u32[]{:S(2)}) copy-start(s32[2,2]{1,0:T(2,128)} %refs_1_.1) | copy-start | bytes 52
  2.3 0.7 %copy-start.2 = (s32[2]{0:T(128)S(1)}, s32[2]{0:T(128)}, u32[]{:S(2)}) copy-start(s32[2]{0:T(128)} %refs_2_.1) | copy-start | bytes 28
  2.9 0.7 %copy-start.3 = (s32[16]{0:T(128)S(1)}, s32[16]{0:T(128)}, u32[]{:S(2)}) copy-start(s32[16]{0:T(128)} %refs_3_.1) | copy-start | bytes 196
  3.6 0.7 %copy-start.4 = (f32[48]{0:T(128)S(1)}, f32[48]{0:T(128)}, u32[]{:S(2)}) copy-start(f32[48]{0:T(128)} %refs_4_.1) | copy-start | bytes 580
  4.2 0.7 %copy-start.5 = (f32[31]{0:T(128)S(1)}, f32[31]{0:T(128)}, u32[]{:S(2)}) copy-start(f32[31]{0:T(128)} %refs_5_.1) | copy-start | bytes 376
  4.9 0.7 %copy-start.6 = (f32[31]{0:T(128)S(1)}, f32[31]{0:T(128)}, u32[]{:S(2)}) copy-start(f32[31]{0:T(128)} %refs_6_.1) | copy-start | bytes 376
  5.5 0.7 %copy-start.7 = (f32[31]{0:T(128)S(1)}, f32[31]{0:T(128)}, u32[]{:S(2)}) copy-start(f32[31]{0:T(128)} %refs_7_.1) | copy-start | bytes 376

commit v3 on v2

--- a/solution.py
+++ b/solution.py
@@ -123,7 +123,18 @@
 
 
 def exact_dot(left, right):
-    return jnp.dot(left, right, precision=lax.Precision.HIGHEST, preferred_element_type=jnp.float32)
+    def halves(value):
+        high = value.astype(jnp.bfloat16)
+        return high, (value - high.astype(jnp.float32)).astype(jnp.bfloat16)
+
+    def product(a, b):
+        return jnp.dot(a, b, preferred_element_type=jnp.float32)
+
+    left_high, left_low = halves(left)
+    right_high, right_low = halves(right)
+    return (
+        product(left_high, right_low) + product(left_low, right_high)
+    ) + product(left_high, right_high)
 
 
 def store_toeplitz(row, position, pieces):
@@ -184,8 +195,9 @@
 
 
 def plane_kernel(
-    n, wide, mask_ref, coords_ref, weights_ref, focus_ref, taps_ref, blur_x_ref, blur_y_ref,
-    blur_z_ref, intensity_ref, latent_ref, rows, t0, t1, t2, t3, stacked, fields, pupils, blur,
+    n, wide, mask_hbm, coords_hbm, weights_hbm, focus_hbm, taps_hbm, blur_x_hbm, blur_y_hbm,
+    blur_z_hbm, intensity_ref, latent_ref, mask_ref, coords_ref, weights_ref, focus_ref, taps_ref,
+    blur_x_ref, blur_y_ref, blur_z_ref, arg_sems, rows, t0, t1, t2, t3, stacked, fields, pupils, blur,
     centre, mix, own, points, points_smem, along, columns, mixed, planes, send_sems, recv_sems,
     local_sem,
 ):
@@ -229,7 +241,26 @@
     def sent(phase, source, target):
         each(lambda off: copy(phase, source, target, off, me).wait_send())
 
+    fetches = [
+        pltpu.make_async_copy(source, target, arg_sems.at[place])
+        for place, (source, target) in enumerate(
+            (
+                (coords_hbm, coords_ref),
+                (weights_hbm, weights_ref),
+                (focus_hbm, focus_ref),
+                (taps_hbm, taps_ref),
+                (blur_x_hbm, blur_x_ref),
+                (blur_y_hbm, blur_y_ref),
+                (blur_z_hbm, blur_z_ref),
+                (mask_hbm, mask_ref),
+            )
+        )
+    ]
+    for fetch in fetches:
+        fetch.start()
     each(signal)
+    for fetch in fetches:
+        fetch.wait()
     lane = lax.broadcasted_iota(jnp.int32, (1, 128), 1)
     packed = jnp.zeros((1, 128), jnp.int32)
     for s in range(local):
@@ -279,7 +310,7 @@
     tall = jnp.broadcast_to(back_y, (16, lanes))
     before = pltpu.roll(tall, lanes - 31, 1, stride=1, stride_axis=0)[:, :256]
     after = pltpu.roll(tall, 241, 1, stride=1, stride_axis=0)[:, :256]
-    pad = jnp.zeros((240, 256), jnp.float32)
+    pad = jnp.zeros((112, 256), jnp.float32)
     distance = lax.broadcasted_iota(jnp.int32, (256, 256), 0) - lax.broadcasted_iota(
         jnp.int32, (256, 256), 1
     )
@@ -289,14 +320,16 @@
 
     receive(1, column_source, columns)
     stack = columns[...].reshape(256, 256)
-    zero = jnp.zeros((wide, 256), jnp.float32)
+    zero = jnp.zeros((wide, 128), jnp.float32)
     along_y = (
         exact_dot(stack, centre[...])
         + exact_dot(
-            jnp.concatenate([zero, stack[:-wide]], axis=0), jnp.concatenate([pad, before], axis=0)
+            jnp.concatenate([zero, stack[:-wide, 128:]], axis=0),
+            jnp.concatenate([pad, before], axis=0),
         )
         + exact_dot(
-            jnp.concatenate([stack[wide:], zero], axis=0), jnp.concatenate([after, pad], axis=0)
+            jnp.concatenate([stack[wide:, :128], zero], axis=0),
+            jnp.concatenate([after, pad], axis=0),
         )
     )
     mixed[...] = exact_dot(mix[...], along_y).reshape(n, wide, 256)
@@ -319,13 +352,18 @@
     full = pltpu.VMEM((256, 256), jnp.float32)
     parts = pltpu.VMEM((n, wide, 256), jnp.float32)
     vmem = pl.BlockSpec(memory_space=pltpu.VMEM)
-    smem = pl.BlockSpec(memory_space=pltpu.SMEM)
+    hbm = pl.BlockSpec(memory_space=pltpu.HBM)
+    arguments = (
+        source_coords, source_weights, focus_steps, pupil_taps, blur_x, blur_y, blur_z
+    )
     return pl.pallas_call(
         lambda *refs: plane_kernel(n, wide, *refs),
         out_shape=(square, square),
-        in_specs=[vmem] + [smem] * 7,
+        in_specs=[hbm] * 8,
         out_specs=(vmem, vmem),
-        scratch_shapes=[pltpu.VMEM((8, lanes), jnp.float32)]
+        scratch_shapes=[pltpu.VMEM((256, 256), jnp.int32)]
+        + [pltpu.SMEM(value.shape, value.dtype) for value in arguments]
+        + [pltpu.SemaphoreType.DMA((8,)), pltpu.VMEM((8, lanes), jnp.float32)]
         + [pltpu.VMEM((24, lanes), jnp.float32)] * 4
         + [
             pltpu.VMEM((512, 256), jnp.bfloat16),
@@ -346,11 +384,9 @@
             pltpu.SemaphoreType.DMA,
         ],
         compiler_params=pltpu.CompilerParams(
-            vmem_limit_bytes=48 * 2**20, collective_id=0, has_side_effects=True
+            vmem_limit_bytes=64 * 2**20 - 2**17, collective_id=0, has_side_effects=True
         ),
-    )(
-        layout_mask, source_coords, source_weights, focus_steps, pupil_taps, blur_x, blur_y, blur_z
-    )
+    )(layout_mask, *arguments)
 
 
 def solution(mesh):

time: 46.1 us -> 40.9 us (0.89)
  local copies, waits for them, and re-layouts: 6.96 us -> 2.42 us
  Pallas kernels: 38.3 us -> 37.7 us
    unnamed x18 -> x4, local copies, waits for them, and re-layouts: 6.96 us -> 2.42 us
    pallas_call x1, Pallas kernels: 38.3 us -> 37.7 us  [plane_per_device(): pl.pallas_call(lambda *refs: plane_kernel(n, wide, *refs), out_shape=(squ...]
where the time goes in v3:
time: 40.9 us; the launch traced here: 40.7 us
  Pallas kernels  37.7 us (92%)
  local copies, waits for them, and re-layouts  2.42 us (6%)
  between operations  0.65 us (2%)
    pallas_call x1, Pallas kernels, plane_per_device(): pl.pallas_call(lambda *refs: plane_kernel(n, wide, *refs), out_shape=(squ...  37.7 us
    unnamed x4, local copies, waits for them, and re-layouts  2.42 us

profile of v3, /device:TPU:0, one launch (start us, length us, event | category | flops | bytes accessed | tf_op | source)
XLA Modules:
  0.0 40.7 jit_solution(14117540418736757235)
XLA Ops:
  0.6 37.7 %shard_map.95 = (f32[256,256]{1,0:T(8,128)}, f32[256,256]{1,0:T(8,128)}) custom-call(s32[256,256]{1,0:T(8,128)} %refs_0_.1, s32[2,2]{1,0:T(2,128)} %refs_1_.1, s32[2]{0:T(128)} %refs_2_.1, s32[16]{0:T(128)} %refs_3_.1, f32[48]{0:T(128)} %refs_4_.1, f32[31]{0:T(128)} %refs_5_.1, f32[31]{0:T(128)} %refs_6_.1, f32[31]{0:T(128)} %refs_7_.1), custom_call_target="tpu_custom_call" | custom-call | tf_op jit(solution)/shard_map/pallas_call | solution.py:359
  38.3 0.0 copy-start
  38.3 1.7 %copy.12 = f32[256,256]{1,0:T(8,128)} copy(f32[256,256]{1,0:T(8,128)} %get-tuple-element.4) | data formatting | bytes 524288
  40.0 0.0 copy-done
  40.0 0.7 %copy.13 = f32[256,256]{1,0:T(8,128)} copy(f32[256,256]{1,0:T(8,128)S(1)} %copy-done) | data formatting | bytes 524288
Async XLA Ops:
  38.3 1.7 %copy-start = (f32[256,256]{1,0:T(8,128)S(1)}, f32[256,256]{1,0:T(8,128)}, u32[]{:S(2)}) copy-start(f32[256,256]{1,0:T(8,128)} %get-tuple-element.5) | copy-start | bytes 786436

commit v4 on v3

--- a/solution.py
+++ b/solution.py
@@ -165,13 +165,14 @@
     imag_ref[:, :128] = amplitude * jnp.sin(phase)
 
 
-def build_tables(tap_count, mask_ref, rows_ref, focus, tap_refs, stacked, fields, pupils):
+def build_tables(tap_count, mask_ref, rows_ref, focus, tap_refs, stacked_slots, fields, pupils):
     forward_real, forward_imag, back_real, back_imag = tap_refs
     store_taps(rows_ref, 0, focus, 1.0, forward_real, forward_imag, tap_count)
     store_taps(rows_ref, 1, focus, -1.0, back_real, back_imag, tap_count)
     mask_bf = mask_ref[...].astype(jnp.float32).astype(jnp.bfloat16)
 
-    def one_shift(shift, carry):
+    def one_shift(shift, slot):
+        stacked = stacked_slots.at[slot]
         row = pl.ds(shift, 1)
         store_toeplitz(forward_real[row, :], 232, ((stacked, 0, 0, 1),))
         store_toeplitz(forward_imag[row, :], 232, ((stacked, 256, 0, 1),))
@@ -181,9 +182,14 @@
         pupil = pupils.at[shift]
         store_toeplitz(back_real[row, :], 233, ((pupil, 0, 0, 1), (pupil, 256, 256, 1)))
         store_toeplitz(back_imag[row, :], 233, ((pupil, 0, 256, 1), (pupil, 256, 0, -1)))
+
+    def two_shifts(pair, carry):
+        one_shift(2 * pair, 0)
+        one_shift(2 * pair + 1, 1)
         return carry
 
-    lax.fori_loop(0, shifts, one_shift, 0)
+    lax.fori_loop(0, shifts // 2, two_shifts, 0)
+    one_shift(shifts - 1, 0)
 
 
 def lane_row(count, value):
@@ -286,8 +292,10 @@
     to_smem.start()
     to_smem.wait()
 
-    def one_device(device, carry):
-        for s in range(local):
+    def two_devices(pair, carry):
+        power = jnp.zeros((256, 256), jnp.float32)
+        for place in range(2 * local):
+            device, s = 2 * pair + place // local, place % local
             point = [points_smem[device, 0, 3 * s + item] for item in range(3)]
             factor = point[2].astype(jnp.float32) / (4.0 * local * n)
             field = jnp.dot(
@@ -295,10 +303,11 @@
                 pupils[point[0] + max_shift],
                 preferred_element_type=jnp.float32,
             )
-            intensity_ref[...] += factor * (field[:, :256] ** 2 + field[:, 256:] ** 2)
+            power = power + factor * (field[:, :256] ** 2 + field[:, 256:] ** 2)
+        intensity_ref[...] += power
         return carry
 
-    lax.fori_loop(0, n, one_device, 0)
+    lax.fori_loop(0, n // 2, two_devices, 0)
     acid = 1.0 - jnp.exp(-dose_scale * intensity_ref[...])
     along[...] = exact_dot(blur[...], acid.T).reshape(n, wide, 256)
     column_source = lambda off: along.at[lax.rem(me + off, n)]
@@ -366,7 +375,7 @@
         + [pltpu.SemaphoreType.DMA((8,)), pltpu.VMEM((8, lanes), jnp.float32)]
         + [pltpu.VMEM((24, lanes), jnp.float32)] * 4
         + [
-            pltpu.VMEM((512, 256), jnp.bfloat16),
+            pltpu.VMEM((2, 512, 256), jnp.bfloat16),
             pltpu.VMEM((shifts, 256, 512), jnp.bfloat16),
             pltpu.VMEM((shifts, 512, 512), jnp.bfloat16),
             full,

time: 40.9 us -> 38.5 us (0.941)
  Pallas kernels: 37.7 us -> 35.2 us
    pallas_call x1, Pallas kernels: 37.7 us -> 35.2 us  [plane_per_device(): pl.pallas_call(lambda *refs: plane_kernel(n, wide, *refs), out_shape=(squ...]
where the time goes in v4:
time: 38.5 us; the launch traced here: 38.3 us
  Pallas kernels  35.2 us (91%)
  local copies, waits for them, and re-layouts  2.42 us (6%)
  between operations  0.65 us (2%)
    pallas_call x1, Pallas kernels, plane_per_device(): pl.pallas_call(lambda *refs: plane_kernel(n, wide, *refs), out_shape=(squ...  35.2 us
    unnamed x4, local copies, waits for them, and re-layouts  2.42 us

profile of v4, /device:TPU:0, one launch (start us, length us, event | category | flops | bytes accessed | tf_op | source)
XLA Modules:
  0.0 38.3 jit_solution(15977388436500347474)
XLA Ops:
  0.6 35.2 %shard_map.95 = (f32[256,256]{1,0:T(8,128)}, f32[256,256]{1,0:T(8,128)}) custom-call(s32[256,256]{1,0:T(8,128)} %refs_0_.1, s32[2,2]{1,0:T(2,128)} %refs_1_.1, s32[2]{0:T(128)} %refs_2_.1, s32[16]{0:T(128)} %refs_3_.1, f32[48]{0:T(128)} %refs_4_.1, f32[31]{0:T(128)} %refs_5_.1, f32[31]{0:T(128)} %refs_6_.1, f32[31]{0:T(128)} %refs_7_.1), custom_call_target="tpu_custom_call" | custom-call | tf_op jit(solution)/shard_map/pallas_call | solution.py:368
  35.9 0.0 copy-start
  35.9 1.7 %copy.12 = f32[256,256]{1,0:T(8,128)} copy(f32[256,256]{1,0:T(8,128)} %get-tuple-element.4) | data formatting | bytes 524288
  37.6 0.0 copy-done
  37.6 0.7 %copy.13 = f32[256,256]{1,0:T(8,128)} copy(f32[256,256]{1,0:T(8,128)S(1)} %copy-done) | data formatting | bytes 524288
Async XLA Ops:
  35.9 1.7 %copy-start = (f32[256,256]{1,0:T(8,128)S(1)}, f32[256,256]{1,0:T(8,128)}, u32[]{:S(2)}) copy-start(f32[256,256]{1,0:T(8,128)} %get-tuple-element.5) | copy-start | bytes 786436

commit v5 on v4

--- a/solution.py
+++ b/solution.py
@@ -183,12 +183,12 @@
         store_toeplitz(back_real[row, :], 233, ((pupil, 0, 0, 1), (pupil, 256, 256, 1)))
         store_toeplitz(back_imag[row, :], 233, ((pupil, 0, 256, 1), (pupil, 256, 0, -1)))
 
-    def two_shifts(pair, carry):
-        one_shift(2 * pair, 0)
-        one_shift(2 * pair + 1, 1)
+    def four_shifts(step, carry):
+        for slot in range(4):
+            one_shift(4 * step + slot, slot)
         return carry
 
-    lax.fori_loop(0, shifts // 2, two_shifts, 0)
+    lax.fori_loop(0, shifts // 4, four_shifts, 0)
     one_shift(shifts - 1, 0)
 
 
@@ -292,10 +292,10 @@
     to_smem.start()
     to_smem.wait()
 
-    def two_devices(pair, carry):
+    def four_devices(step, carry):
         power = jnp.zeros((256, 256), jnp.float32)
-        for place in range(2 * local):
-            device, s = 2 * pair + place // local, place % local
+        for place in range(4 * local):
+            device, s = 4 * step + place // local, place % local
             point = [points_smem[device, 0, 3 * s + item] for item in range(3)]
             factor = point[2].astype(jnp.float32) / (4.0 * local * n)
             field = jnp.dot(
@@ -307,7 +307,7 @@
         intensity_ref[...] += power
         return carry
 
-    lax.fori_loop(0, n // 2, two_devices, 0)
+    lax.fori_loop(0, n // 4, four_devices, 0)
     acid = 1.0 - jnp.exp(-dose_scale * intensity_ref[...])
     along[...] = exact_dot(blur[...], acid.T).reshape(n, wide, 256)
     column_source = lambda off: along.at[lax.rem(me + off, n)]
@@ -375,7 +375,7 @@
         + [pltpu.SemaphoreType.DMA((8,)), pltpu.VMEM((8, lanes), jnp.float32)]
         + [pltpu.VMEM((24, lanes), jnp.float32)] * 4
         + [
-            pltpu.VMEM((2, 512, 256), jnp.bfloat16),
+            pltpu.VMEM((4, 512, 256), jnp.bfloat16),
             pltpu.VMEM((shifts, 256, 512), jnp.bfloat16),
             pltpu.VMEM((shifts, 512, 512), jnp.bfloat16),
             full,

time: 38.5 us -> 38.2 us (level)
  no operation moved by 1% of the time
where the time goes in v5:
time: 38.2 us; the launch traced here: 38.1 us
  Pallas kernels  35 us (92%)
  local copies, waits for them, and re-layouts  2.42 us (6%)
  between operations  0.65 us (2%)
    pallas_call x1, Pallas kernels, plane_per_device(): pl.pallas_call(lambda *refs: plane_kernel(n, wide, *refs), out_shape=(squ...  35 us
    unnamed x4, local copies, waits for them, and re-layouts  2.42 us

profile of v5, /device:TPU:0, one launch (start us, length us, event | category | flops | bytes accessed | tf_op | source)
XLA Modules:
  0.0 38.1 jit_solution(8440749675412489477)
XLA Ops:
  0.6 35.0 %shard_map.95 = (f32[256,256]{1,0:T(8,128)}, f32[256,256]{1,0:T(8,128)}) custom-call(s32[256,256]{1,0:T(8,128)} %refs_0_.1, s32[2,2]{1,0:T(2,128)} %refs_1_.1, s32[2]{0:T(128)} %refs_2_.1, s32[16]{0:T(128)} %refs_3_.1, f32[48]{0:T(128)} %refs_4_.1, f32[31]{0:T(128)} %refs_5_.1, f32[31]{0:T(128)} %refs_6_.1, f32[31]{0:T(128)} %refs_7_.1), custom_call_target="tpu_custom_call" | custom-call | tf_op jit(solution)/shard_map/pallas_call | solution.py:368
  35.7 0.0 copy-start
  35.7 1.7 %copy.12 = f32[256,256]{1,0:T(8,128)} copy(f32[256,256]{1,0:T(8,128)} %get-tuple-element.4) | data formatting | bytes 524288
  37.4 0.0 copy-done
  37.4 0.7 %copy.13 = f32[256,256]{1,0:T(8,128)} copy(f32[256,256]{1,0:T(8,128)S(1)} %copy-done) | data formatting | bytes 524288
Async XLA Ops:
  35.7 1.7 %copy-start = (f32[256,256]{1,0:T(8,128)S(1)}, f32[256,256]{1,0:T(8,128)}, u32[]{:S(2)}) copy-start(f32[256,256]{1,0:T(8,128)} %get-tuple-element.5) | copy-start | bytes 786436

commit v6 on v5

--- a/solution.py
+++ b/solution.py
@@ -138,16 +138,25 @@
 
 
 def store_toeplitz(row, position, pieces):
-    base = pltpu.roll(jnp.broadcast_to(row, (16, lanes)), position, 1, stride=1, stride_axis=0)
+    base = pltpu.roll(jnp.broadcast_to(row, (16, 128)), 0, 1, stride=1, stride_axis=0)
+    lane = lax.broadcasted_iota(jnp.int32, (16, 128), 1)
+    zero = jnp.zeros((16, 128), jnp.float32)
     for j in range(8):
-        rolled = pltpu.roll(base, lanes - 128 + 16 * j, 1)
-        for block, start in ((j + 8, 0), (j, 128)):
-            part = rolled[:, start : start + 256]
-            for ref, top, side, sign in pieces:
-                value = part if sign > 0 else -part
-                ref[top + 16 * block : top + 16 * block + 16, side : side + 256] = value.astype(
-                    ref.dtype
-                )
+        first = 16 * j + position - 256
+        turn, tile = first % 128, first // 128
+        rolled = pltpu.roll(base, turn, 1) if turn else base
+        wraps = turn > 65
+        kept = jnp.where(lane >= turn, rolled, zero) if wraps else rolled
+        wrapped = jnp.where(lane < turn, rolled, zero) if wraps else zero
+        for block, start in ((j, tile), (j + 8, tile + 1)):
+            for column in range(2):
+                part = kept if column == start else wrapped if column == start + 1 else zero
+                for ref, top, side, sign in pieces:
+                    value = part if sign > 0 else -part
+                    left = side + 128 * column
+                    ref[top + 16 * block : top + 16 * block + 16, left : left + 128] = (
+                        value.astype(ref.dtype)
+                    )
 
 
 def store_taps(taps_ref, row, focus, flip, real_ref, imag_ref, tap_count):
@@ -159,10 +168,8 @@
     phase = (
         two_pi * tilt * relative / tap_count + defocus_scale * focus * (relative / centre) ** 2
     )
-    real_ref[...] = jnp.zeros_like(real_ref)
-    imag_ref[...] = jnp.zeros_like(imag_ref)
-    real_ref[:, :128] = amplitude * jnp.cos(phase)
-    imag_ref[:, :128] = amplitude * jnp.sin(phase)
+    real_ref[...] = amplitude * jnp.cos(phase)
+    imag_ref[...] = amplitude * jnp.sin(phase)
 
 
 def build_tables(tap_count, mask_ref, rows_ref, focus, tap_refs, stacked_slots, fields, pupils):
@@ -285,7 +292,7 @@
 
     focus = focus_ref[me].astype(jnp.float32)
     build_tables(tap_count, mask_ref, rows, focus, (t0, t1, t2, t3), stacked, fields, pupils)
-    store_toeplitz(rows[2:3, :], 241, ((blur, 0, 0, 1),))
+    store_toeplitz(rows[2:3, :128], 241, ((blur, 0, 0, 1),))
     intensity_ref[...] = jnp.zeros_like(intensity_ref)
     receive(0, point_source, points)
     to_smem = pltpu.make_async_copy(points, points_smem, local_sem)
@@ -315,7 +322,7 @@
     columns[me] = along[me]
 
     back_y = rows[3:4, :]
-    store_toeplitz(back_y, 241, ((centre, 0, 0, 1),))
+    store_toeplitz(rows[3:4, :128], 241, ((centre, 0, 0, 1),))
     tall = jnp.broadcast_to(back_y, (16, lanes))
     before = pltpu.roll(tall, lanes - 31, 1, stride=1, stride_axis=0)[:, :256]
     after = pltpu.roll(tall, 241, 1, stride=1, stride_axis=0)[:, :256]
@@ -373,7 +380,7 @@
         scratch_shapes=[pltpu.VMEM((256, 256), jnp.int32)]
         + [pltpu.SMEM(value.shape, value.dtype) for value in arguments]
         + [pltpu.SemaphoreType.DMA((8,)), pltpu.VMEM((8, lanes), jnp.float32)]
-        + [pltpu.VMEM((24, lanes), jnp.float32)] * 4
+        + [pltpu.VMEM((24, 128), jnp.float32)] * 4
         + [
             pltpu.VMEM((4, 512, 256), jnp.bfloat16),
             pltpu.VMEM((shifts, 256, 512), jnp.bfloat16),

time: 38.2 us -> 35.6 us (0.932)
  Pallas kernels: 35 us -> 32.3 us
    pallas_call x1, Pallas kernels: 35 us -> 32.3 us  [plane_per_device(): pl.pallas_call(lambda *refs: plane_kernel(n, wide, *refs), out_shape=(squ...]
where the time goes in v6:
time: 35.6 us; the launch traced here: 35.4 us
  Pallas kernels  32.3 us (91%)
  local copies, waits for them, and re-layouts  2.42 us (7%)
  between operations  0.65 us (2%)
    pallas_call x1, Pallas kernels, plane_per_device(): pl.pallas_call(lambda *refs: plane_kernel(n, wide, *refs), out_shape=(squ...  32.3 us
    unnamed x4, local copies, waits for them, and re-layouts  2.42 us

profile of v6, /device:TPU:0, one launch (start us, length us, event | category | flops | bytes accessed | tf_op | source)
XLA Modules:
  0.0 35.4 jit_solution(4053038512303646562)
XLA Ops:
  0.6 32.3 %shard_map.95 = (f32[256,256]{1,0:T(8,128)}, f32[256,256]{1,0:T(8,128)}) custom-call(s32[256,256]{1,0:T(8,128)} %refs_0_.1, s32[2,2]{1,0:T(2,128)} %refs_1_.1, s32[2]{0:T(128)} %refs_2_.1, s32[16]{0:T(128)} %refs_3_.1, f32[48]{0:T(128)} %refs_4_.1, f32[31]{0:T(128)} %refs_5_.1, f32[31]{0:T(128)} %refs_6_.1, f32[31]{0:T(128)} %refs_7_.1), custom_call_target="tpu_custom_call" | custom-call | tf_op jit(solution)/shard_map/pallas_call | solution.py:375
  33.0 0.0 copy-start
  33.0 1.7 %copy.12 = f32[256,256]{1,0:T(8,128)} copy(f32[256,256]{1,0:T(8,128)} %get-tuple-element.4) | data formatting | bytes 524288
  34.7 0.0 copy-done
  34.7 0.7 %copy.13 = f32[256,256]{1,0:T(8,128)} copy(f32[256,256]{1,0:T(8,128)S(1)} %copy-done) | data formatting | bytes 524288
Async XLA Ops:
  33.0 1.7 %copy-start = (f32[256,256]{1,0:T(8,128)S(1)}, f32[256,256]{1,0:T(8,128)}, u32[]{:S(2)}) copy-start(f32[256,256]{1,0:T(8,128)} %get-tuple-element.5) | copy-start | bytes 786436

commit v7 on v6

--- a/solution.py
+++ b/solution.py
@@ -137,7 +137,7 @@
     ) + product(left_high, right_high)
 
 
-def store_toeplitz(row, position, pieces):
+def store_toeplitz(row, position, pieces, apart=128):
     base = pltpu.roll(jnp.broadcast_to(row, (16, 128)), 0, 1, stride=1, stride_axis=0)
     lane = lax.broadcasted_iota(jnp.int32, (16, 128), 1)
     zero = jnp.zeros((16, 128), jnp.float32)
@@ -153,7 +153,7 @@
                 part = kept if column == start else wrapped if column == start + 1 else zero
                 for ref, top, side, sign in pieces:
                     value = part if sign > 0 else -part
-                    left = side + 128 * column
+                    left = side + apart * column
                     ref[top + 16 * block : top + 16 * block + 16, left : left + 128] = (
                         value.astype(ref.dtype)
                     )
@@ -187,8 +187,8 @@
         fields[shift, :, :256] = first[:256].astype(jnp.bfloat16)
         fields[shift, :, 256:] = first[256:].astype(jnp.bfloat16)
         pupil = pupils.at[shift]
-        store_toeplitz(back_real[row, :], 233, ((pupil, 0, 0, 1), (pupil, 256, 256, 1)))
-        store_toeplitz(back_imag[row, :], 233, ((pupil, 0, 256, 1), (pupil, 256, 0, -1)))
+        store_toeplitz(back_real[row, :], 233, ((pupil, 0, 0, 1), (pupil, 256, 128, 1)), 256)
+        store_toeplitz(back_imag[row, :], 233, ((pupil, 0, 128, 1), (pupil, 256, 0, -1)), 256)
 
     def four_shifts(step, carry):
         for slot in range(4):
@@ -241,18 +241,31 @@
             device_id_type=pl.DeviceIdType.MESH,
         )
 
-    def start(phase, source, target):
-        each(lambda off: copy(phase, source, target, off, me).start())
-
-    def receive(phase, source, target):
+    def block_of(device):
+        return device // 2 + lax.rem(device, 2) * (n // 2)
+
+    def itself(device):
+        return device
+
+    def start(phase, source, target, place=itself, wanted=None):
+        def one(off):
+            transfer = copy(phase, source, target, off, place(me))
+            if wanted is None:
+                transfer.start()
+            else:
+                pl.when(wanted(block_of(lax.rem(me + off, n))))(transfer.start)
+
+        each(one)
+
+    def receive(phase, source, target, place=itself):
         each(
             lambda off: copy(
-                phase, source, target, off, lax.rem(me + n - off, n)
+                phase, source, target, off, place(lax.rem(me + n - off, n))
             ).wait_recv()
         )
 
-    def sent(phase, source, target):
-        each(lambda off: copy(phase, source, target, off, me).wait_send())
+    def sent(phase, source, target, place=itself):
+        each(lambda off: copy(phase, source, target, off, place(me)).wait_send())
 
     fetches = [
         pltpu.make_async_copy(source, target, arg_sems.at[place])
@@ -299,27 +312,40 @@
     to_smem.start()
     to_smem.wait()
 
-    def four_devices(step, carry):
-        power = jnp.zeros((256, 256), jnp.float32)
-        for place in range(4 * local):
-            device, s = 4 * step + place // local, place % local
-            point = [points_smem[device, 0, 3 * s + item] for item in range(3)]
-            factor = point[2].astype(jnp.float32) / (4.0 * local * n)
-            field = jnp.dot(
-                fields[point[1] + max_shift],
-                pupils[point[0] + max_shift],
-                preferred_element_type=jnp.float32,
-            )
-            power = power + factor * (field[:, :256] ** 2 + field[:, 256:] ** 2)
-        intensity_ref[...] += power
-        return carry
-
-    lax.fori_loop(0, n // 4, four_devices, 0)
-    acid = 1.0 - jnp.exp(-dose_scale * intensity_ref[...])
-    along[...] = exact_dot(blur[...], acid.T).reshape(n, wide, 256)
-    column_source = lambda off: along.at[lax.rem(me + off, n)]
-    start(1, column_source, columns)
-    columns[me] = along[me]
+    def image_half(half):
+        def four_devices(step, carry):
+            power = jnp.zeros((256, 128), jnp.float32)
+            for place in range(4 * local):
+                device, s = 4 * step + place // local, place % local
+                point = [points_smem[device, 0, 3 * s + item] for item in range(3)]
+                factor = point[2].astype(jnp.float32) / (4.0 * local * n)
+                field = jnp.dot(
+                    fields[point[1] + max_shift],
+                    pupils[point[0] + max_shift, :, 256 * half : 256 * half + 256],
+                    preferred_element_type=jnp.float32,
+                )
+                power = power + factor * (field[:, :128] ** 2 + field[:, 128:] ** 2)
+            intensity_ref[:, 128 * half : 128 * half + 128] += power
+            return carry
+
+        lax.fori_loop(0, n // 4, four_devices, 0)
+
+    def acid_columns(stop):
+        return (1.0 - jnp.exp(-dose_scale * intensity_ref[:, :stop])).T
+
+    early = (128 - blur_count // 2) // wide
+    column_source = lambda off: along.at[block_of(lax.rem(me + off, n))]
+    image_half(0)
+    along[:early] = exact_dot(blur[: early * wide, :128], acid_columns(128)).reshape(
+        early, wide, 256
+    )
+    start(1, column_source, columns, wanted=lambda block: block < early)
+    image_half(1)
+    along[early:] = exact_dot(blur[early * wide :, :], acid_columns(256)).reshape(
+        n - early, wide, 256
+    )
+    start(1, column_source, columns, wanted=lambda block: block >= early)
+    columns[me] = along[block_of(me)]
 
     back_y = rows[3:4, :]
     store_toeplitz(rows[3:4, :128], 241, ((centre, 0, 0, 1),))
@@ -350,13 +376,13 @@
     )
     mixed[...] = exact_dot(mix[...], along_y).reshape(n, wide, 256)
     plane_source = lambda off: mixed.at[lax.rem(me + off, n)]
-    start(2, plane_source, planes)
-    planes[me] = mixed[me]
+    start(2, plane_source, planes, block_of)
+    planes[block_of(me)] = mixed[me]
     sent(0, point_source, points)
     sent(1, column_source, columns)
-    receive(2, plane_source, planes)
+    receive(2, plane_source, planes, block_of)
     latent_ref[...] = planes[...].reshape(256, 256).T
-    sent(2, plane_source, planes)
+    sent(2, plane_source, planes, block_of)
 
 
 def plane_per_device(

time: 35.6 us -> 34.5 us (0.969)
  Pallas kernels: 32.3 us -> 31.3 us
    pallas_call x1, Pallas kernels: 32.3 us -> 31.3 us  [plane_per_device(): pl.pallas_call(lambda *refs: plane_kernel(n, wide, *refs), out_shape=(squ...]
where the time goes in v7:
time: 34.5 us; the launch traced here: 34.4 us
  Pallas kernels  31.3 us (91%)
  local copies, waits for them, and re-layouts  2.42 us (7%)
  between operations  0.65 us (2%)
    pallas_call x1, Pallas kernels, plane_per_device(): pl.pallas_call(lambda *refs: plane_kernel(n, wide, *refs), out_shape=(squ...  31.3 us
    unnamed x4, local copies, waits for them, and re-layouts  2.42 us

profile of v7, /device:TPU:0, one launch (start us, length us, event | category | flops | bytes accessed | tf_op | source)
XLA Modules:
  0.0 34.4 jit_solution(4760234390805929670)
XLA Ops:
  0.6 31.3 %shard_map.95 = (f32[256,256]{1,0:T(8,128)}, f32[256,256]{1,0:T(8,128)}) custom-call(s32[256,256]{1,0:T(8,128)} %refs_0_.1, s32[2,2]{1,0:T(2,128)} %refs_1_.1, s32[2]{0:T(128)} %refs_2_.1, s32[16]{0:T(128)} %refs_3_.1, f32[48]{0:T(128)} %refs_4_.1, f32[31]{0:T(128)} %refs_5_.1, f32[31]{0:T(128)} %refs_6_.1, f32[31]{0:T(128)} %refs_7_.1), custom_call_target="tpu_custom_call" | custom-call | tf_op jit(solution)/shard_map/pallas_call | solution.py:401
  32.0 0.0 copy-start
  32.0 1.7 %copy.12 = f32[256,256]{1,0:T(8,128)} copy(f32[256,256]{1,0:T(8,128)} %get-tuple-element.4) | data formatting | bytes 524288
  33.7 0.0 copy-done
  33.7 0.7 %copy.13 = f32[256,256]{1,0:T(8,128)} copy(f32[256,256]{1,0:T(8,128)S(1)} %copy-done) | data formatting | bytes 524288
Async XLA Ops:
  32.0 1.7 %copy-start = (f32[256,256]{1,0:T(8,128)S(1)}, f32[256,256]{1,0:T(8,128)}, u32[]{:S(2)}) copy-start(f32[256,256]{1,0:T(8,128)} %get-tuple-element.5) | copy-start | bytes 786436

commit v8 on v7

--- a/solution.py
+++ b/solution.py
@@ -248,7 +248,8 @@
         return device
 
     def start(phase, source, target, place=itself, wanted=None):
-        def one(off):
+        def one(turn):
+            off = lax.rem(turn + n // 2 - 2, n - 1) + 1
             transfer = copy(phase, source, target, off, place(me))
             if wanted is None:
                 transfer.start()

time: 34.5 us -> 37.6 us (1.090)
  Pallas kernels: 31.3 us -> 34.4 us
    pallas_call x1, Pallas kernels: 31.3 us -> 34.4 us  [plane_per_device(): pl.pallas_call(lambda *refs: plane_kernel(n, wide, *refs), out_shape=(squ...]
where the time goes in v8:
time: 37.6 us; the launch traced here: 37.4 us
  Pallas kernels  34.4 us (91%)
  local copies, waits for them, and re-layouts  2.42 us (6%)
  between operations  0.65 us (2%)
    pallas_call x1, Pallas kernels, plane_per_device(): pl.pallas_call(lambda *refs: plane_kernel(n, wide, *refs), out_shape=(squ...  34.4 us
    unnamed x4, local copies, waits for them, and re-layouts  2.42 us

profile of v8, /device:TPU:0, one launch (start us, length us, event | category | flops | bytes accessed | tf_op | source)
XLA Modules:
  0.0 37.4 jit_solution(14733567651121215520)
XLA Ops:
  0.6 34.4 %shard_map.95 = (f32[256,256]{1,0:T(8,128)}, f32[256,256]{1,0:T(8,128)}) custom-call(s32[256,256]{1,0:T(8,128)} %refs_0_.1, s32[2,2]{1,0:T(2,128)} %refs_1_.1, s32[2]{0:T(128)} %refs_2_.1, s32[16]{0:T(128)} %refs_3_.1, f32[48]{0:T(128)} %refs_4_.1, f32[31]{0:T(128)} %refs_5_.1, f32[31]{0:T(128)} %refs_6_.1, f32[31]{0:T(128)} %refs_7_.1), custom_call_target="tpu_custom_call" | custom-call | tf_op jit(solution)/shard_map/pallas_call | solution.py:402
  35.0 0.0 copy-start
  35.0 1.7 %copy.12 = f32[256,256]{1,0:T(8,128)} copy(f32[256,256]{1,0:T(8,128)} %get-tuple-element.4) | data formatting | bytes 524288
  36.7 0.0 copy-done
  36.7 0.7 %copy.13 = f32[256,256]{1,0:T(8,128)} copy(f32[256,256]{1,0:T(8,128)S(1)} %copy-done) | data formatting | bytes 524288
Async XLA Ops:
  35.0 1.7 %copy-start = (f32[256,256]{1,0:T(8,128)S(1)}, f32[256,256]{1,0:T(8,128)}, u32[]{:S(2)}) copy-start(f32[256,256]{1,0:T(8,128)} %get-tuple-element.5) | copy-start | bytes 786436
